TPU v7x, 32 devices: a whole 2x2x4 slice. The times are simulated.
32 devices in a mesh: group: 8 (over z, y), inner: 4 (over x, core).
Axes of the slice: x: 2, y: 2, z: 4, core: 2. Of those that a mesh axis runs over, the one named last changes fastest.
Arguments:
- inputs: bfloat16 [32768, 768], P(('group', 'inner')), may hold values from -6 to 6
- upstream: bfloat16 [32768, 768], P(('group', 'inner')), may hold values from -6 to 6
- buckets: int32 [32], P(('group', 'inner')), may hold values from 0 to 1
- lengths: int32 [32, 8], P(('group', 'inner')), may hold values from 32 to 128
- layer_keep: int32 [32, 8], P(('group', 'inner')), may hold values 0 or 1
- attend_weight: bfloat16 [768, 2304], P(('group', 'inner')), may hold values from -0.21875 to 0.21875
- attend_bias: bfloat16 [1536], P(('group', 'inner')), may hold values from -1.796875 to 1.796875
- merge_weight: bfloat16 [768, 768], P(('group', 'inner')), may hold values from -1.75 to 1.75
- merge_bias: bfloat16 [768], P(('group', 'inner')), may hold values from -1.796875 to 1.796875
- expand_weight: bfloat16 [768, 3072], P(('group', 'inner')), may hold values from -0.21875 to 0.21875
- expand_bias: bfloat16 [3072], P(('group', 'inner')), may hold values from -3 to 3
- shrink_weight: bfloat16 [3072, 768], P(('group', 'inner')), may hold values from -0.21875 to 0.21875
- shrink_bias: bfloat16 [768], P(('group', 'inner')), may hold values from -1.796875 to 1.796875
- norm_gain: bfloat16 [2, 768], P(None, ('group', 'inner')), may hold values from 0.5 to 1.5
- norm_shift: bfloat16 [2, 768], P(None, ('group', 'inner')), may hold values from -1.796875 to 1.796875
Outputs:
- outputs: bfloat16 [32768, 768], P(('group', 'inner'))
- input_grad: float32 [32768, 768], P(('group', 'inner'))
- attend_weight_grad: float32 [768, 2304], P(('group', 'inner'))
- attend_bias_grad: float32 [1536], P(('group', 'inner'))
- merge_weight_grad: float32 [768, 768], P(('group', 'inner'))
- merge_bias_grad: float32 [768], P(('group', 'inner'))
- expand_weight_grad: float32 [768, 3072], P(('group', 'inner'))
- expand_bias_grad: float32 [3072], P(('group', 'inner'))
- shrink_weight_grad: float32 [3072, 768], P(('group', 'inner'))
- shrink_bias_grad: float32 [768], P(('group', 'inner'))
- norm_gain_grad: float32 [2, 768], P(None, ('group', 'inner'))
- norm_shift_grad: float32 [2, 768], P(None, ('group', 'inner'))
All inputs are finite; a program needn't handle non-finite values. No bound on the sum of `layer_keep` on one device may be relied on, other than what follows from the above.
Results may differ from a plain program's by a relative error of at most 0.014.
Values may be sent and summed in bfloat16 or wider, within the bound.
A program may use at most 192 MiB of HBM per device.

v0:
```python
import jax
import jax.numpy as jnp
from jax import lax
from jax.sharding import PartitionSpec as P

HEADS = 12
HD = 64
LONG = 512
SHORT = 128
TOK_DEV = 1024
SLOTS = 8


epsilon = 1e-05
masked_score = -1e30


def layer_norm(hidden, gains, shifts):
    center = hidden - jnp.mean(hidden, axis=-1, keepdims=True)
    spread = jnp.mean(center * center, axis=-1, keepdims=True)
    return center * lax.rsqrt(spread + epsilon) * gains + shifts


def gelu_exact(values):
    return jax.nn.gelu(values, approximate=False)


def matmul(left, right):
    return jnp.dot(left, right, preferred_element_type=jnp.float32)


def token_info(bucket, slot_lengths, slot_keeps):
    position = jnp.arange(TOK_DEV, dtype=jnp.int32)
    span_size = jnp.where(bucket > 0, LONG, SHORT).astype(jnp.int32)
    sequence = position // span_size
    within = position - sequence * span_size
    slot_index = sequence * (span_size // SHORT)
    matches = (slot_index[:, None] == jnp.arange(SLOTS, dtype=jnp.int32)[None, :]).astype(jnp.int32)
    length = jnp.sum(matches * slot_lengths[None, :], axis=1) + bucket * (LONG - SHORT)
    keep_flags = jnp.sum(matches * slot_keeps[None, :], axis=1)
    return (sequence, within < length, keep_flags > 0)


def masked_scores(queries, key_rows, sequence, valid_key):
    scores = jnp.einsum("qhd,khd->hqk", queries, key_rows, preferred_element_type=jnp.float32)
    allowed = (sequence[:, None] == sequence[None, :]) & valid_key[None, :]
    return jnp.where(allowed[None], scores, masked_score)


def attend_block(pieces):
    queries, key_rows, values, sequence, valid_key = pieces
    scores = masked_scores(queries, key_rows, sequence, valid_key)
    highest = jnp.max(scores, axis=-1, keepdims=True)
    raised = jnp.exp(scores - highest)
    row_total = jnp.sum(raised, axis=-1, keepdims=True)
    weights = raised / row_total
    mixed_rows = jnp.einsum(
        "hqk,khd->qhd", weights.astype(jnp.bfloat16), values, preferred_element_type=jnp.float32
    )
    return (mixed_rows, highest[:, :, 0] + jnp.log(row_total[:, :, 0]))


def attend_back(pieces):
    queries, key_rows, values, sequence, valid_key, logsum, mixed_grad = pieces
    scores = masked_scores(queries, key_rows, sequence, valid_key)
    weights = jnp.exp(scores - logsum[:, :, None])
    weight_grad = jnp.einsum("qhd,khd->hqk", mixed_grad, values, preferred_element_type=jnp.float32)
    row_dot = jnp.sum(weights * weight_grad, axis=-1, keepdims=True)
    score_grad = (weights * (weight_grad - row_dot)).astype(jnp.bfloat16)
    query_part = jnp.einsum(
        "hqk,khd->qhd", score_grad, key_rows, preferred_element_type=jnp.float32
    ).astype(jnp.bfloat16)
    key_part = jnp.einsum(
        "hqk,qhd->khd", score_grad, queries, preferred_element_type=jnp.float32
    ).astype(jnp.bfloat16)
    value_part = jnp.einsum(
        "hqk,qhd->khd", weights.astype(jnp.bfloat16), mixed_grad, preferred_element_type=jnp.float32
    ).astype(jnp.bfloat16)
    return (query_part, key_part, value_part)


def heads_view(source):
    return source.reshape(source.shape[0] // LONG, LONG, HEADS, HD)


def forward_pass(inputs, weights, sequence, valid_key, keep_flags):
    (
        attend_matrix,
        attend_offset,
        merge_matrix,
        merge_offset,
        expand_matrix,
        expand_offset,
        shrink_matrix,
        shrink_offset,
        gains,
        shifts,
    ) = weights
    model_width = inputs.shape[1]
    blocks = inputs.shape[0] // LONG
    packed = matmul(inputs, attend_matrix)
    offset = attend_offset.astype(jnp.float32)
    queries = ((packed[:, :model_width] + offset[:model_width]) * 0.125).astype(jnp.bfloat16)
    key_rows = packed[:, model_width : 2 * model_width].astype(jnp.bfloat16)
    values = (packed[:, 2 * model_width :] + offset[model_width:]).astype(jnp.bfloat16)
    mixed_rows, logsum = lax.map(
        attend_block,
        (
            heads_view(queries),
            heads_view(key_rows),
            heads_view(values),
            sequence.reshape(blocks, LONG),
            valid_key.reshape(blocks, LONG),
        ),
    )
    mixed_rows = mixed_rows.reshape(-1, model_width).astype(jnp.bfloat16)
    tokens = inputs.astype(jnp.float32)
    first_sum = tokens + matmul(mixed_rows, merge_matrix) + merge_offset.astype(jnp.float32)
    normed = layer_norm(first_sum, gains[0].astype(jnp.float32), shifts[0].astype(jnp.float32))
    normed_low = normed.astype(jnp.bfloat16)
    expanded = matmul(normed_low, expand_matrix) + expand_offset.astype(jnp.float32)
    active = gelu_exact(expanded).astype(jnp.bfloat16)
    second_sum = normed + matmul(active, shrink_matrix) + shrink_offset.astype(jnp.float32)
    result = layer_norm(second_sum, gains[1].astype(jnp.float32), shifts[1].astype(jnp.float32))
    outputs = jnp.where(keep_flags[:, None], result, tokens).astype(jnp.bfloat16)
    return (
        outputs,
        (
            queries,
            key_rows,
            values,
            logsum,
            mixed_rows,
            first_sum,
            normed_low,
            expanded,
            active,
            second_sum,
        ),
    )


def backward_pass(inputs, upstream, weights, saved, sequence, valid_key, keep_flags):
    (
        attend_matrix,
        attend_offset,
        merge_matrix,
        merge_offset,
        expand_matrix,
        expand_offset,
        shrink_matrix,
        shrink_offset,
        gains,
        shifts,
    ) = weights
    (
        queries,
        key_rows,
        values,
        logsum,
        mixed_rows,
        first_sum,
        normed_low,
        expanded,
        active,
        second_sum,
    ) = saved
    model_width = inputs.shape[1]
    blocks = inputs.shape[0] // LONG
    cotangent = upstream.astype(jnp.float32)
    result_grad = jnp.where(keep_flags[:, None], cotangent, 0.0)
    second_out, pull_second = jax.vjp(
        layer_norm, second_sum, gains[1].astype(jnp.float32), shifts[1].astype(jnp.float32)
    )
    second_grad, gain_two, shift_two = pull_second(result_grad)
    shrink_in = second_grad.astype(jnp.bfloat16)
    shrink_grad = jnp.einsum("tf,td->fd", active, shrink_in, preferred_element_type=jnp.float32)
    shrink_offset_grad = jnp.sum(shrink_in.astype(jnp.float32), axis=0)
    active_grad = jnp.einsum(
        "td,fd->tf", shrink_in, shrink_matrix, preferred_element_type=jnp.float32
    )
    gelu_out, pull_gelu = jax.vjp(gelu_exact, expanded)
    expand_in = pull_gelu(active_grad)[0].astype(jnp.bfloat16)
    expand_grad = jnp.einsum("td,tf->df", normed_low, expand_in, preferred_element_type=jnp.float32)
    expand_offset_grad = jnp.sum(expand_in.astype(jnp.float32), axis=0)
    normed_grad = second_grad + jnp.einsum(
        "tf,df->td", expand_in, expand_matrix, preferred_element_type=jnp.float32
    )
    first_out, pull_first = jax.vjp(
        layer_norm, first_sum, gains[0].astype(jnp.float32), shifts[0].astype(jnp.float32)
    )
    first_grad, gain_one, shift_one = pull_first(normed_grad)
    branch_in = first_grad.astype(jnp.bfloat16)
    merge_grad = jnp.einsum("td,te->de", mixed_rows, branch_in, preferred_element_type=jnp.float32)
    merge_offset_grad = jnp.sum(branch_in.astype(jnp.float32), axis=0)
    mixed_grad = jnp.einsum(
        "te,de->td", branch_in, merge_matrix, preferred_element_type=jnp.float32
    ).astype(jnp.bfloat16)
    query_part, key_part, value_part = lax.map(
        attend_back,
        (
            heads_view(queries),
            heads_view(key_rows),
            heads_view(values),
            sequence.reshape(blocks, LONG),
            valid_key.reshape(blocks, LONG),
            logsum,
            heads_view(mixed_grad),
        ),
    )
    query_grad = query_part.reshape(-1, model_width) * 0.125
    packed_grad = jnp.concatenate(
        [query_grad, key_part.reshape(-1, model_width), value_part.reshape(-1, model_width)], axis=1
    )
    attend_grad = jnp.einsum("td,te->de", inputs, packed_grad, preferred_element_type=jnp.float32)
    attend_offset_grad = jnp.concatenate(
        [
            jnp.sum(query_grad.astype(jnp.float32), axis=0),
            jnp.sum(value_part.reshape(-1, model_width).astype(jnp.float32), axis=0),
        ]
    )
    input_grad = (
        first_grad
        + jnp.einsum("te,de->td", packed_grad, attend_matrix, preferred_element_type=jnp.float32)
        + jnp.where(keep_flags[:, None], 0.0, cotangent)
    )
    gain_grad = jnp.stack([gain_one, gain_two])
    shift_grad = jnp.stack([shift_one, shift_two])
    grads = (
        attend_grad,
        attend_offset_grad,
        merge_grad,
        merge_offset_grad,
        expand_grad,
        expand_offset_grad,
        shrink_grad,
        shrink_offset_grad,
        gain_grad,
        shift_grad,
    )
    return (grads, input_grad)


def on_device(
    inputs,
    upstream,
    buckets,
    lengths,
    layer_keep,
    attend_weight,
    attend_bias,
    merge_weight,
    merge_bias,
    expand_weight,
    expand_bias,
    shrink_weight,
    shrink_bias,
    norm_gain,
    norm_shift,
):
    sequence, valid_key, keep_flags = token_info(buckets[0], lengths[0], layer_keep[0])
    gathered = (
        lax.all_gather(attend_weight, ("group", "inner"), axis=0, tiled=True),
        lax.all_gather(attend_bias, ("group", "inner"), axis=0, tiled=True),
        lax.all_gather(merge_weight, ("group", "inner"), axis=0, tiled=True),
        lax.all_gather(merge_bias, ("group", "inner"), axis=0, tiled=True),
        lax.all_gather(expand_weight, ("group", "inner"), axis=0, tiled=True),
        lax.all_gather(expand_bias, ("group", "inner"), axis=0, tiled=True),
        lax.all_gather(shrink_weight, ("group", "inner"), axis=0, tiled=True),
        lax.all_gather(shrink_bias, ("group", "inner"), axis=0, tiled=True),
        lax.all_gather(norm_gain, ("group", "inner"), axis=1, tiled=True),
        lax.all_gather(norm_shift, ("group", "inner"), axis=1, tiled=True),
    )
    outputs, saved = forward_pass(inputs, gathered, sequence, valid_key, keep_flags)
    gathered = (
        lax.all_gather(attend_weight, ("group", "inner"), axis=0, tiled=True),
        lax.all_gather(attend_bias, ("group", "inner"), axis=0, tiled=True),
        lax.all_gather(merge_weight, ("group", "inner"), axis=0, tiled=True),
        lax.all_gather(merge_bias, ("group", "inner"), axis=0, tiled=True),
        lax.all_gather(expand_weight, ("group", "inner"), axis=0, tiled=True),
        lax.all_gather(expand_bias, ("group", "inner"), axis=0, tiled=True),
        lax.all_gather(shrink_weight, ("group", "inner"), axis=0, tiled=True),
        lax.all_gather(shrink_bias, ("group", "inner"), axis=0, tiled=True),
        lax.all_gather(norm_gain, ("group", "inner"), axis=1, tiled=True),
        lax.all_gather(norm_shift, ("group", "inner"), axis=1, tiled=True),
    )
    grads, input_grad = backward_pass(
        inputs, upstream, gathered, saved, sequence, valid_key, keep_flags
    )
    shares = (
        lax.psum_scatter(grads[0], ("group", "inner"), scatter_dimension=0, tiled=True),
        lax.psum_scatter(grads[1], ("group", "inner"), scatter_dimension=0, tiled=True),
        lax.psum_scatter(grads[2], ("group", "inner"), scatter_dimension=0, tiled=True),
        lax.psum_scatter(grads[3], ("group", "inner"), scatter_dimension=0, tiled=True),
        lax.psum_scatter(grads[4], ("group", "inner"), scatter_dimension=0, tiled=True),
        lax.psum_scatter(grads[5], ("group", "inner"), scatter_dimension=0, tiled=True),
        lax.psum_scatter(grads[6], ("group", "inner"), scatter_dimension=0, tiled=True),
        lax.psum_scatter(grads[7], ("group", "inner"), scatter_dimension=0, tiled=True),
        lax.psum_scatter(grads[8], ("group", "inner"), scatter_dimension=1, tiled=True),
        lax.psum_scatter(grads[9], ("group", "inner"), scatter_dimension=1, tiled=True),
    )
    return (
        outputs,
        input_grad,
        shares[0],
        shares[1],
        shares[2],
        shares[3],
        shares[4],
        shares[5],
        shares[6],
        shares[7],
        shares[8],
        shares[9],
    )


def solution(mesh):
    placed = (
        P(("group", "inner"), None),
        P(("group", "inner"), None),
        P(("group", "inner")),
        P(("group", "inner"), None),
        P(("group", "inner"), None),
        P(("group", "inner"), None),
        P(("group", "inner")),
        P(("group", "inner"), None),
        P(("group", "inner")),
        P(("group", "inner"), None),
        P(("group", "inner")),
        P(("group", "inner"), None),
        P(("group", "inner")),
        P(None, ("group", "inner")),
        P(None, ("group", "inner")),
    )
    return jax.shard_map(
        on_device,
        mesh=mesh,
        in_specs=placed,
        out_specs=(
            P(("group", "inner"), None),
            P(("group", "inner"), None),
            P(("group", "inner"), None),
            P(("group", "inner")),
            P(("group", "inner"), None),
            P(("group", "inner")),
            P(("group", "inner"), None),
            P(("group", "inner")),
            P(("group", "inner"), None),
            P(("group", "inner")),
            P(None, ("group", "inner")),
            P(None, ("group", "inner")),
        ),
        check_vma=False,
    )
```

profile of v0, /device:TPU:0, one launch (start us, length us, event | category | flops | bytes accessed | tf_op | source)
XLA Modules:
  0.0 838.9 jit_solution(11787737680824837263)
XLA Ops:
  15.5 42.4 %all-reduce.11 = (bf16[1536]{0:T(1024)(128)(2,1)S(1)}, bf16[768]{0:T(1024)(128)(2,1)S(1)}, bf16[3072]{0:T(1024)(128)(2,1)S(1)}, bf16[768]{0:T(1024)(128)(2,1)S(1)}) all-reduce(bf16[1536]{0:T(1024)(128)(2,1)S(1)} %dynamic-update-slice, bf16[768]{0:T(1024)(128)(2,1)S(1)} %dynamic-update-slice.1, ...), channel_id=1, replica_groups=mesh['group'=8,'inner'=4] {'group','inner'}, use_global_device_ids=true, to_apply=%add | all-reduce | flops 6144 | bytes 24576
  57.9 2.8 copy.105
  60.7 40.0 %all-gather = bf16[32,24,2]{1,2,0:T(2,128)(2,1)S(1)} all-gather(bf16[1,24,2]{1,2,0:T(2,128)(2,1)S(1)} %bitcast.191), channel_id=1, replica_groups=mesh['group'=8,'inner'=4] {'group','inner'}, dimensions={0}, use_global_device_ids=true | all-gather | bytes 3168 | tf_op jit(solution)/shard_map/all_gather | solution.py:271
  101.4 36.4 %all-gather.1 = bf16[32,24,2]{1,2,0:T(2,128)(2,1)S(1)} all-gather(bf16[1,24,2]{1,2,0:T(2,128)(2,1)S(1)} %bitcast.192), channel_id=1, replica_groups=mesh['group'=8,'inner'=4] {'group','inner'}, dimensions={0}, use_global_device_ids=true | all-gather | bytes 3168 | tf_op jit(solution)/shard_map/all_gather | solution.py:272
  141.3 5.8 fusion.91
  147.3 2.3 fusion.70
  149.5 1.7 copy.106
  151.3 2.4 reshape.281
  153.7 2.9 copy.109
  156.5 1.7 copy.107
  158.3 2.4 reshape.282
  160.7 1.7 copy.110
  162.4 1.6 copy.108
  164.0 3.9 reshape.283
  167.9 1.7 copy.111
  169.6 19.4 %while.26 = (s32[]{:T(128)}, bf16[2,512,12,64]{1,3,2,0:T(8,128)(2,1)}, f32[2,12,512]{2,1,0:T(8,128)S(1)}, bf16[2,512,12,64]{1,3,2,0:T(8,128)(2,1)}, s32[2,512]{1...) while((s32[]{:T(128)}, ...), condition=%wide.region_5.6_spmd, body=%wide.region_2.5_spmd.sunk | while | flops 834136064 | bytes 42960488 | solution.py:106
  170.2 1.9 select_reduce_fusion.4
  172.1 2.2 fusion.133
  174.3 5.1 bitcast_dynamic-update-slice_fusion.4
  179.7 1.9 select_reduce_fusion.4
  181.7 2.2 fusion.133
  183.9 5.1 bitcast_dynamic-update-slice_fusion.4
  189.0 4.2 copy.112
  194.9 3.8 fusion.89
  199.2 38.3 %multiply_convert_fusion.1 = (bf16[1024,3072]{1,0:T(8,128)(2,1)}, f32[1024,3072]{1,0:T(8,128)}, f32[1024,3072]{1,0:T(8,128)}) fusion(f32[3072]{0:T(1024)S(1)} %convert_element_type.115, bf16[768,3072]{1,0:T(8,128)(2,1)} %all-gather.11.cloned.1.call-done, f32[1024,768]{0,1:T(8,128)S(1)} %get-tuple-element.325, f32[768]{0:T(1024)S(1)} %get-tuple-element.256, ...), kind=kOutput, calls=%fused_computation.67 | convolution fusion | flops 5043388416 | bytes 39348224 | tf_op jit(solution)/shard_map/dot_general | solution.py:29
  237.4 22.9 %all-gather.13.cloned.1.call-done = bf16[3072,768]{1,0:T(8,128)(2,1)} async-done(((bf16[96,768]{1,0:T(8,128)(2,1)}), bf16[3072,768]{1,0:T(8,128)(2,1)}) %all-gather.13.cloned.1.call-update) | async-done | bytes 4718608 | tf_op jit(solution)/shard_map/all_gather | solution.py:269
  260.4 9.7 %fusion.90 = (f32[1024]{0:T(1024)S(1)}, f32[1024,768]{0,1:T(8,128)S(1)}) fusion(f32[768]{0:T(1024)S(1)} %copy-done.55, bf16[1024,3072]{1,0:T(8,128)(2,1)} %get-tuple-element.311, bf16[3072,768]{1,0:T(8,128)(2,1)} %all-gather.13.cloned.1.call-done, f32[768]{0:T(1024)S(1)} %get-tuple-element.256, f32[768]{0:T(1024)S(1)} %get-tuple-element.254, ...), kind=kOutput, calls=%fused_computation.165 | convolution fusion | flops 4837342208 | bytes 17323008 | tf_op jit(solution)/shard_map/dot_general | solution.py:29
  270.1 1.7 fusion.64
  271.8 2.0 fusion.67
  273.8 3.7 convert_reduce_fusion.1
  277.5 18.2 %convert_reduce_fusion = (f32[3072]{0:T(1024)}, bf16[1024,3072]{1,0:T(8,128)(2,1)}) fusion(f32[1024,3072]{1,0:T(8,128)} %get-tuple-element.312, bf16[1024,768]{0,1:T(8,128)(2,1)S(1)} %get-tuple-element.306, bf16[3072,768]{1,0:T(8,128)(2,1)} %all-gather.13.cloned.1.call-done, f32[1024,3072]{1,0:T(8,128)} %get-tuple-element.326, ...), kind=kOutput, calls=%fused_computation.65 | convolution fusion | flops 4885312512 | bytes 37773312 | tf_op jit(solution)/shard_map/td,fd->tf/dot_general | solution.py:179
  295.7 11.7 %multiply_reduce_fusion.1 = (f32[768]{0:T(1024)}, f32[1024]{0:T(1024)S(1)}, f32[768]{0:T(1024)}, f32[1024,768]{0,1:T(8,128)S(1)}) fusion(f32[1024,768]{0,1:T(8,128)} %copy-done.9, f32[1024]{0:T(1024)S(1)} %fusion.75, f32[1024]{0:T(1024)S(1)} %broadcast_multiply_fusion.2, f32[768]{0:T(1024)S(1)} %get-tuple-element.254, ...), kind=kOutput, calls=%fused_computation.104 | convolution fusion | flops 4845990912 | bytes 22062080 | tf_op jit(solution)/shard_map/tf,df->td/dot_general | solution.py:186
  307.5 2.4 fusion.86
  310.5 2.8 convert_reduce_fusion.2
  313.3 2.9 fusion.92
  316.2 2.7 convolution_convert_fusion.2
  319.7 2.4 reshape.284
  322.0 3.0 copy.120
  325.2 48.7 %while.27 = (s32[]{:T(128)}, bf16[2,512,12,64]{1,3,2,0:T(8,128)(2,1)}, bf16[2,512,12,64]{1,3,2,0:T(8,128)(2,1)}, bf16[2,512,12,64]{1,3,2,0:T(8,128)(2,1)}, bf16[...) while((s32[]{:T(128)}, ...), condition=%wide.region_16.17_spmd, body=%wide.region_14.16_spmd.sunk | while | flops 2052712448 | bytes 147526480 | solution.py:199
  325.9 1.8 fusion.142
  327.8 6.6 multiply_reduce_fusion.6
  334.5 7.2 multiply_convert_fusion.3
  341.7 2.0 fusion.144
  346.1 3.6 fusion.145
  350.0 1.8 fusion.142
  351.9 6.6 multiply_reduce_fusion.6
  358.6 7.2 multiply_convert_fusion.3
  365.8 2.0 fusion.144
  370.1 3.6 fusion.145
  375.5 1.6 copy.122
  377.5 1.6 copy.123
  382.0 2.1 copy-done.27
  384.2 5.8 convolution_bitcast_fusion
  389.9 8.0 copy.135
  398.0 1.8 copy-done.11
  399.8 10.6 %fusion.81 = f32[768,3072]{1,0:T(8,128)} fusion(bf16[1024,3072]{1,0:T(8,128)(2,1)} %get-tuple-element.331, f32[1024,768]{0,1:T(8,128)S(1)} %copy-done.11, f32[768]{0:T(1024)S(1)} %copy-done.52, f32[768]{0:T(1024)S(1)} %copy-done.38, f32[1024]{0:T(1024)S(1)} %copy-done.46, f32[1024]{0:T(1024)S(1)} %copy-done.36), kind=kOutput, calls=%fused_computation.159 | convolution fusion | flops 4835770368 | bytes 18888704 | tf_op jit(solution)/shard_map/td,tf->df/dot_general | solution.py:184
  411.8 10.4 %fusion.93 = f32[3072,768]{1,0:T(8,128)} fusion(bf16[1024,3072]{1,0:T(8,128)(2,1)} %get-tuple-element.311, bf16[1024,768]{0,1:T(8,128)(2,1)S(1)} %copy-done.26), kind=kOutput, calls=%fused_computation.168 | convolution fusion | flops 4831838208 | bytes 17301504 | tf_op jit(solution)/shard_map/tf,td->fd/dot_general | solution.py:177
  423.7 2.0 convert_reduce_fusion.3
  425.9 40.4 %all-reduce.10 = (f32[1536]{0:T(1024)S(1)}, f32[768]{0:T(1024)S(1)}, f32[3072]{0:T(1024)S(1)}, f32[768]{0:T(1024)S(1)}, f32[2,768]{1,0:T(2,128)S(1)}, /*index=5*/f32[2,768]{1,0:T(2,128)S(1)}) all-reduce(f32[1536]{0:T(1024)S(1)} %pad_maximum_fusion, ...), channel_id=3, replica_groups=mesh['group'=8,'inner'=4] {'group','inner'}, use_global_device_ids=true, to_apply=%region_20.21.clone | all-reduce | flops 9216 | bytes 73728
  467.5 10.2 %fusion.68 = f32[1024,768]{0,1:T(8,128)} fusion(bf16[1024,768]{0,1:T(8,128)(2,1)S(1)} %copy-done.5, f32[1024,768]{0,1:T(8,128)} %get-tuple-element.310, bf16[768,2304]{1,0:T(8,128)(2,1)} %all-gather.7.cloned.1.call-done, bf16[1024,2304]{0,1:T(8,128)(2,1)} %copy-done.27, f32[1024]{0:T(1024)S(1)} %copy-done.44, pred[1024]{0:T(1024)(128)(4,1)S(1)} %copy-done.49), kind=kOutput, calls=%fused_computation.97 | convolution fusion | flops 3627810816 | bytes 16126976 | tf_op jit(solution)/shard_map/te,de->td/dot_general | solution.py:224
  477.7 3.9 copy.127
  485.6 62.6 %reduce-scatter.15.cloned.1.call-done = f32[24,2304]{1,0:T(8,128)} async-done(((f32[768,2304]{1,0:T(8,128)}), f32[24,2304]{1,0:T(8,128)}) %reduce-scatter.15.cloned.1.call-update) | async-done | bytes 221200
  548.2 141.3 %reduce-scatter.11.cloned.1.call-done = f32[24,3072]{1,0:T(8,128)} async-done(((f32[768,3072]{1,0:T(8,128)}), f32[24,3072]{1,0:T(8,128)}) %reduce-scatter.11.cloned.1.call-update) | async-done | bytes 294928 | tf_op jit(solution)/shard_map/reduce_scatter | solution.py:295
  689.5 142.3 %reduce-scatter.13.cloned.1.call-done = f32[96,768]{1,0:T(8,128)} async-done(((f32[3072,768]{1,0:T(8,128)}), f32[96,768]{1,0:T(8,128)}) %reduce-scatter.13.cloned.1.call-update) | async-done | bytes 294928 | tf_op jit(solution)/shard_map/reduce_scatter | solution.py:297
  (231 shorter events, 34.2 us)
Async XLA Ops:
  7.2 53.5 %copy-start.56 = (bf16[2,24]{1,0:T(2,128)(2,1)S(1)}, bf16[2,24]{1,0:T(2,128)(2,1)}, u32[]{:S(2)}) copy-start(bf16[2,24]{1,0:T(2,128)(2,1)} %param.32) | copy-start | bytes 292
  7.2 94.2 %copy-start.57 = (bf16[2,24]{1,0:T(2,128)(2,1)S(1)}, bf16[2,24]{1,0:T(2,128)(2,1)}, u32[]{:S(2)}) copy-start(bf16[2,24]{1,0:T(2,128)(2,1)} %param.33) | copy-start | bytes 292
  7.2 132.5 %copy-start.18 = (bf16[1024,768]{1,0:T(8,128)(2,1)S(1)}, bf16[1024,768]{1,0:T(8,128)(2,1)}, u32[]{:S(2)}) copy-start(bf16[1024,768]{1,0:T(8,128)(2,1)} %param.20) | copy-start | bytes 4718596
  7.2 134.1 %all-gather.7.cloned.1.call-start = ((), (), s32[]{:S(2)}) async-start(), calls=%async_computation.4 | async-start | bytes 3649536 | tf_op jit(solution)/shard_map/all_gather | solution.py:263
  7.9 186.9 %all-gather.9.cloned.1.call-start = ((), (), s32[]{:S(2)}) async-start(), calls=%async_computation.5 | async-start | bytes 1216512 | tf_op jit(solution)/shard_map/all_gather | solution.py:265
  8.7 190.5 %all-gather.11.cloned.1.call-start = ((), (), s32[]{:S(2)}) async-start(), calls=%async_computation.6 | async-start | bytes 4866048 | tf_op jit(solution)/shard_map/all_gather | solution.py:267
  9.4 250.9 %all-gather.13.cloned.1.call-start = ((), (), s32[]{:S(2)}) async-start(), calls=%async_computation.7 | async-start | bytes 4866048 | tf_op jit(solution)/shard_map/all_gather | solution.py:269
  10.0 475.6 %reduce-scatter.9.cloned.1.call-start = ((), (), s32[]{:S(2)}) async-start(), calls=%async_computation.8 | async-start | bytes 2433024 | tf_op jit(solution)/shard_map/reduce_scatter | solution.py:293
  57.9 83.4 %copy-start.19 = (bf16[1024,768]{1,0:T(8,128)(2,1)S(1)}, bf16[1024,768]{1,0:T(8,128)(2,1)}, u32[]{:S(2)}) copy-start(bf16[1024,768]{1,0:T(8,128)(2,1)} %param.19) | copy-start | bytes 4718596
  101.4 206.0 %copy-start.37 = (f32[768]{0:T(1024)}, f32[768]{0:T(1024)S(1)}, u32[]{:S(2)}) copy-start(f32[768]{0:T(1024)S(1)} %get-tuple-element.254) | copy-start | bytes 9220
  138.5 121.9 %copy-start.51 = (f32[768]{0:T(1024)}, f32[768]{0:T(1024)S(1)}, u32[]{:S(2)}) copy-start(f32[768]{0:T(1024)S(1)} %get-tuple-element.256) | copy-start | bytes 9220
  189.0 5.8 copy-start
  189.0 5.8 copy-start.2
  189.0 5.8 copy-start.28
  189.0 5.8 copy-start.30
  189.0 5.8 copy-start.32
  198.7 38.7 %copy-start.9 = (f32[1024,768]{0,1:T(8,128)}, f32[1024,768]{0,1:T(8,128)S(1)}, u32[]{:S(2)}) copy-start(f32[1024,768]{0,1:T(8,128)S(1)} %get-tuple-element.325) | copy-start | bytes 9437188
  198.7 108.7 %copy-start.35 = (f32[1024]{0:T(1024)}, f32[1024]{0:T(1024)S(1)}, u32[]{:S(2)}) copy-start(f32[1024]{0:T(1024)S(1)} %broadcast_multiply_fusion.2) | copy-start | bytes 12292
  199.1 108.3 %copy-start.45 = (f32[1024]{0:T(1024)}, f32[1024]{0:T(1024)S(1)}, u32[]{:S(2)}) copy-start(f32[1024]{0:T(1024)S(1)} %fusion.75) | copy-start | bytes 12292
  199.2 61.2 %copy-start.55 = (f32[768]{0:T(1024)S(1)}, f32[768]{0:T(1024)}, u32[]{:S(2)}) copy-start(f32[768]{0:T(1024)} %convert_element_type.117) | copy-start | bytes 9220
  260.4 9.7 %copy-start.4 = (bf16[1024,768]{0,1:T(8,128)(2,1)S(1)}, bf16[1024,768]{0,1:T(8,128)(2,1)}, u32[]{:S(2)}) copy-start(bf16[1024,768]{0,1:T(8,128)(2,1)} %copy.115) | copy-start | bytes 4718596
  260.4 9.7 %copy-start.34 = (f32[768]{0:T(1024)S(1)}, f32[768]{0:T(1024)}, u32[]{:S(2)}) copy-start(f32[768]{0:T(1024)} %get-tuple-element.253) | copy-start | bytes 9220
  260.4 9.7 %copy-start.48 = (pred[1024]{0:T(1024)(128)(4,1)S(1)}, pred[1024]{0:T(1024)(128)(4,1)}, u32[]{:S(2)}) copy-start(pred[1024]{0:T(1024)(128)(4,1)} %broadcast_compare_fusion) | copy-start | bytes 3076
  271.8 2.1 copy-start.17
  271.8 2.1 copy-start.41
  277.5 18.2 %copy-start.25 = (bf16[1024,768]{0,1:T(8,128)(2,1)}, bf16[1024,768]{0,1:T(8,128)(2,1)S(1)}, u32[]{:S(2)}) copy-start(bf16[1024,768]{0,1:T(8,128)(2,1)S(1)} %get-tuple-element.306) | copy-start | bytes 4718596
  295.7 11.7 %copy-start.10 = (f32[1024,768]{0,1:T(8,128)S(1)}, f32[1024,768]{0,1:T(8,128)}, u32[]{:S(2)}) copy-start(f32[1024,768]{0,1:T(8,128)} %copy-done.9) | copy-start | bytes 9437188
  309.9 3.4 copy-start.24
  322.0 3.1 copy-start.1
  322.0 3.2 copy-start.3
  322.0 3.2 copy-start.29
  322.0 3.2 copy-start.31
  322.0 3.2 copy-start.33
  325.1 223.1 %reduce-scatter.15.cloned.1.call-start = ((), (), s32[]{:S(2)}) async-start(), calls=%async_computation.11 | async-start | bytes 7299072
  325.9 1.9 copy-start.6
  325.9 1.9 copy-start.7
  334.5 7.2 copy-start.21
  341.7 2.0 copy-start.12
  343.7 2.3 copy-start.8
  350.0 1.9 copy-start.6
  350.0 1.9 copy-start.7
  358.6 7.2 copy-start.21
  365.7 2.0 copy-start.12
  367.8 2.4 copy-start.8
  375.5 2.1 copy-start.23
  377.5 2.1 copy-start.15
  381.8 2.4 copy-start.20
  382.0 2.1 copy-start.27
  397.9 1.9 copy-start.11
  397.9 1.9 copy-start.36
  397.9 1.9 copy-start.38
  397.9 1.9 copy-start.46
  397.9 1.9 copy-start.52
  398.0 291.6 %reduce-scatter.11.cloned.1.call-start = ((), (), s32[]{:S(2)}) async-start(), calls=%async_computation.9 | async-start | bytes 9732096 | tf_op jit(solution)/shard_map/reduce_scatter | solution.py:295
  410.4 1.4 copy-start.26
  410.4 421.4 %reduce-scatter.13.cloned.1.call-start = ((), (), s32[]{:S(2)}) async-start(), calls=%async_computation.10 | async-start | bytes 9732096 | tf_op jit(solution)/shard_map/reduce_scatter | solution.py:297
  422.3 1.4 copy-start.14
  422.3 3.5 copy-start.39
  422.3 3.5 copy-start.40
  422.3 3.5 copy-start.50
  422.3 45.1 %copy-start.5 = (bf16[1024,768]{0,1:T(8,128)(2,1)S(1)}, bf16[1024,768]{0,1:T(8,128)(2,1)}, u32[]{:S(2)}) copy-start(bf16[1024,768]{0,1:T(8,128)(2,1)} %copy.115) | copy-start | bytes 4718596
  422.3 45.1 %copy-start.44 = (f32[1024]{0:T(1024)S(1)}, f32[1024]{0:T(1024)}, u32[]{:S(2)}) copy-start(f32[1024]{0:T(1024)} %copy-done.43) | copy-start | bytes 12292
  422.3 45.1 %copy-start.49 = (pred[1024]{0:T(1024)(128)(4,1)S(1)}, pred[1024]{0:T(1024)(128)(4,1)}, u32[]{:S(2)}) copy-start(pred[1024]{0:T(1024)(128)(4,1)} %broadcast_compare_fusion) | copy-start | bytes 3076
  477.7 3.9 copy-start.16
  (9 other events, 8.1 us)
Sparse Core Ops, SparseCore 0:
  10.9 62.8 all-gather.6
  76.7 52.7 all-gather.8
  132.5 62.6 all-gather.10
  197.9 62.4 all-gather.12
  325.2 97.7 reduce-scatter.8
  430.1 118.0 reduce-scatter.14
  554.7 134.7 reduce-scatter.10
  697.0 134.7 reduce-scatter.12
where the time goes:
time: 848 us; the launch traced here: 839 us
  waiting for transfers between devices  372 us (44%)
  matrix products  175 us (21%)
  blocking collectives  159 us (19%)
  local copies, waits for them, and re-layouts  73.7 us (9%)
  other arithmetic  42.4 us (5%)
  between operations  15.8 us (2%)
    reduce_scatter x1, waiting for transfers between devices, on_device(): lax.psum_scatter(grads[6], ('group', 'inner'), scatter_dimension=0, tiled...  142 us
    reduce_scatter x1, waiting for transfers between devices, on_device(): lax.psum_scatter(grads[4], ('group', 'inner'), scatter_dimension=0, tiled...  141 us
    unnamed x2, blocking collectives  82.8 us
    unnamed x9, waiting for transfers between devices  65.2 us
    dot_general x4, matrix products, matmul(): return jnp.dot(left, right, preferred_element_type=jnp.float32)  57.6 us
    all_gather x1, blocking collectives, on_device(): lax.all_gather(norm_gain, ('group', 'inner'), axis=1, tiled=True)  40 us
    all_gather x1, blocking collectives, on_device(): lax.all_gather(norm_shift, ('group', 'inner'), axis=1, tiled=True)  36.4 us
    unnamed x129, local copies, waits for them, and re-layouts  35.4 us
  transfers between devices with their start and end apart: 8, of which 4 were waited for; matrix products, arithmetic and copies ran while one was open for 26% of the time, Pallas kernels for 0%

commit v1 on v0

--- a/solution.py
+++ b/solution.py
@@ -1,6 +1,8 @@
 import jax
 import jax.numpy as jnp
 from jax import lax
+from jax.experimental import pallas as pl
+from jax.experimental.pallas import tpu as pltpu
 from jax.sharding import PartitionSpec as P
 
 HEADS = 12
@@ -9,11 +11,1126 @@
 SHORT = 128
 TOK_DEV = 1024
 SLOTS = 8
-
-
+D = 768
+FF = 3072
+LANES = 128
 epsilon = 1e-05
 masked_score = -1e30
-
+f32 = jnp.float32
+bf16 = jnp.bfloat16
+
+
+def dot_nn(a, b):
+    return lax.dot_general(a, b, (((1,), (0,)), ((), ())), preferred_element_type=f32)
+
+
+def dot_nt(a, b):
+    return lax.dot_general(a, b, (((1,), (1,)), ((), ())), preferred_element_type=f32)
+
+
+def dot_tn(a, b):
+    return lax.dot_general(a, b, (((0,), (0,)), ((), ())), preferred_element_type=f32)
+
+
+def lane_index(rows):
+    return lax.broadcasted_iota(jnp.int32, (rows, LANES), 1)
+
+
+def token_tables(bucket, lengths, keeps, query_const, key_const, keep_table):
+    shape = (TOK_DEV, LANES)
+    position = lax.broadcasted_iota(jnp.int32, shape, 0)
+    is_long = jnp.broadcast_to(bucket, shape) > 0
+    slot = jnp.where(is_long, (position >> 9) << 2, position >> 7)
+    offset = jnp.where(is_long, position & (LONG - 1), position & (SHORT - 1))
+    length = jnp.zeros(shape, jnp.int32)
+    keep = jnp.zeros(shape, jnp.int32)
+    for b in range(SLOTS):
+        here = slot == b
+        length = jnp.where(here, lengths[b], length)
+        keep = jnp.where(here, keeps[b], keep)
+    length = length + bucket * (LONG - SHORT)
+    valid = offset < length
+    within = jnp.where(is_long, 0, (position >> 7) & 3)
+    lane = lax.broadcasted_iota(jnp.int32, shape, 1) & (HD - 1)
+    is_span = (lane >= 4) & (lane < 8)
+    same = lane - 4 == within
+    zero, one = jnp.zeros(shape, f32), jnp.ones(shape, f32)
+    query_const[...] = jnp.where(lane == 3, one, jnp.where(is_span & ~same, one, zero)).astype(bf16)
+    key_const[...] = jnp.where(
+        lane < 3,
+        one,
+        jnp.where(((lane == 3) & ~valid) | (is_span & same), masked_score * one, zero),
+    ).astype(bf16)
+    keep_table[...] = jnp.where(keep > 0, one, zero)
+
+
+def three_parts(column, rows):
+    wide = jnp.broadcast_to(column, (rows, LANES))
+    high = wide.astype(bf16)
+    rest = wide - high.astype(f32)
+    middle = rest.astype(bf16)
+    low = (rest - middle.astype(f32)).astype(bf16)
+    return high, middle, low
+
+
+def attend_forward(index, query_const, key_const, q_ref, k_ref, v_ref, mixed_ref, logsum_ref, tile):
+    pair, block = index // 2, index % 2
+    cols = pl.ds(pl.multiple_of(pair * LANES, LANES), LANES)
+    rows = pl.ds(pl.multiple_of(block * LONG, LONG), LONG)
+    lane_k = lane_index(LONG)
+    k2, v2 = k_ref[rows, cols], v_ref[rows, cols]
+    kc = key_const[rows, :]
+    k_aug = [jnp.where((lane_k // HD) == half, k2, kc) for half in range(2)]
+    lane_q = lane_index(tile)
+    for t in range(LONG // tile):
+        qrows = pl.ds(pl.multiple_of(block * LONG + t * tile, tile), tile)
+        q2, qc = q_ref[qrows, cols], query_const[qrows, :]
+        outs = []
+        sums = logsum_ref[qrows, :]
+        for half in range(2):
+            q_aug = jnp.where((lane_q // HD) == half, q2, qc)
+            scores = dot_nt(q_aug, k_aug[half])
+            highest = jnp.max(scores, axis=1, keepdims=True)
+            raised = jnp.exp(scores - highest)
+            total = jnp.sum(raised, axis=1, keepdims=True)
+            out = dot_nn(raised.astype(bf16), v2)
+            outs.append(out * (1.0 / total))
+            sums = jnp.where(lane_q == 2 * pair + half, highest + jnp.log(total), sums)
+        logsum_ref[qrows, :] = sums
+        mixed_ref[qrows, cols] = jnp.where(lane_q < HD, outs[0], outs[1]).astype(bf16)
+
+
+def attend_backward(index, query_const, key_const, q_ref, k_ref, v_ref, mixed_ref, logsum_ref, mixed_grad_ref,
+                    dq_ref, dk_ref, dv_ref, tile):
+    pair, block = index // 2, index % 2
+    cols = pl.ds(pl.multiple_of(pair * LANES, LANES), LANES)
+    rows = pl.ds(pl.multiple_of(block * LONG, LONG), LONG)
+    lane = lane_index(LONG)
+    q2, dm2 = q_ref[rows, cols], mixed_grad_ref[rows, cols]
+    product = dm2.astype(f32) * mixed_ref[rows, cols].astype(f32)
+    sums = logsum_ref[rows, :]
+    qc = query_const[rows, :]
+    zero = jnp.zeros((LONG, LANES), bf16)
+    q_aug, d_aug = [], []
+    for half in range(2):
+        mine = (lane // HD) == half
+        at = lane & (HD - 1)
+        logsum = jnp.sum(jnp.where(lane == 2 * pair + half, sums, 0.0), axis=1, keepdims=True)
+        delta = jnp.sum(jnp.where(mine, product, 0.0), axis=1, keepdims=True)
+        lh, lm, ll = three_parts(-logsum, LONG)
+        dh, dm, dl = three_parts(-delta, LONG)
+        extra = jnp.where(at == 0, lh, jnp.where(at == 1, lm, jnp.where(at == 2, ll, qc)))
+        q_aug.append(jnp.where(mine, q2, extra))
+        extra = jnp.where(at == 0, dh, jnp.where(at == 1, dm, jnp.where(at == 2, dl, zero)))
+        d_aug.append(jnp.where(mine, dm2, extra))
+    dq = [jnp.zeros((LONG, LANES), f32) for _ in range(2)]
+    lane_t = lane_index(tile)
+    one = jnp.ones((tile, LANES), bf16)
+    zero_t = jnp.zeros((tile, LANES), bf16)
+    for t in range(LONG // tile):
+        krows = pl.ds(pl.multiple_of(block * LONG + t * tile, tile), tile)
+        k2, v2, kc = k_ref[krows, cols], v_ref[krows, cols], key_const[krows, :]
+        vc = jnp.where((lane_t & (HD - 1)) < 3, one, zero_t)
+        dk, dv = [], []
+        for half in range(2):
+            mine = (lane_t // HD) == half
+            weights = jnp.exp(dot_nt(jnp.where(mine, k2, kc), q_aug[half]))
+            grads = weights * dot_nt(jnp.where(mine, v2, vc), d_aug[half])
+            low, low_grads = weights.astype(bf16), grads.astype(bf16)
+            dv.append(dot_nn(low, dm2))
+            dk.append(dot_nn(low_grads, q2))
+            dq[half] = dq[half] + dot_tn(low_grads, k2)
+        dk_ref[krows, cols] = jnp.where(lane_t < HD, dk[0], dk[1]).astype(bf16)
+        dv_ref[krows, cols] = jnp.where(lane_t < HD, dv[0], dv[1]).astype(bf16)
+    dq_ref[rows, cols] = (jnp.where(lane < HD, dq[0], dq[1]).astype(bf16).astype(f32) * 0.125).astype(bf16)
+
+
+def gelu_parts(x):
+    z = jnp.abs(x) * 0.7071067811865476
+    t = 1.0 / (1.0 + 0.3275911 * z)
+    bell = jnp.exp(-z * z)
+    tail = t * (0.127414796 + t * (-0.142248368 + t * (0.7107068705 + t * (-0.7265760135 + t * 0.5307027145)))) * bell
+    phi = jnp.where(x >= 0.0, 1.0 - tail, tail)
+    return x * phi, phi + x * (bell * 0.3989422804014327)
+
+
+def norm_parts(x):
+    center = x - jnp.mean(x, axis=-1, keepdims=True)
+    spread = jnp.mean(center * center, axis=-1, keepdims=True)
+    rstd = lax.rsqrt(spread + epsilon)
+    return center * rstd, rstd
+
+
+def norm_back(dy_hat, x_hat, rstd):
+    a = jnp.mean(dy_hat, axis=-1, keepdims=True)
+    b = jnp.mean(dy_hat * x_hat, axis=-1, keepdims=True)
+    return rstd * (dy_hat - a - x_hat * b)
+
+MESH = pl.DeviceIdType.MESH
+Z, X, Y = 4, 2, 2
+CHIPS = Z * Y * X
+JOBS = 6
+PART = FF // JOBS
+BLOCK = D // CHIPS
+FF_BLOCK = FF // CHIPS
+SLICE = FF_BLOCK // JOBS
+
+
+class Place:
+    def __init__(self):
+        group, inner = lax.axis_index("group"), lax.axis_index("inner")
+        self.z, self.y, self.x, self.c = group // Y, group % Y, inner // 2, inner % 2
+        self.index = group * (X * 2) + inner
+        self.chip = group * X + self.x
+        self.twin = (group, self.x * 2 + 1 - self.c)
+        self.over_x = (group, (1 - self.x) * 2 + self.c)
+        self.over_y = (self.z * Y + 1 - self.y, inner)
+        self.other_z = (self.z + 1 - 2 * (self.z % 2), (self.z + 2) % Z, Z - 1 - self.z)
+        self.over_z = tuple((z * Y + self.y, inner) for z in self.other_z)
+
+    def greet(self):
+        barrier = pltpu.get_barrier_semaphore()
+        peers = (self.twin, self.over_x, self.over_y) + self.over_z
+        for peer in peers:
+            pl.semaphore_signal(barrier, 1, device_id=peer, device_id_type=MESH)
+        pl.semaphore_wait(barrier, len(peers))
+
+
+def remote(source, target, send, recv, peer):
+    return pltpu.make_async_remote_copy(
+        src_ref=source, dst_ref=target, send_sem=send, recv_sem=recv, device_id=peer, device_id_type=MESH
+    )
+
+
+def aligned(value, unit):
+    return pl.multiple_of(value, unit)
+
+
+class Cut:
+    def __init__(self, rows, cols, first=None, near=(slice(None), slice(None))):
+        self.rows, self.cols, self.first, self.near = rows, cols, first, near
+
+
+def row_parts(start, low, high, cols):
+    return (
+        Cut(pl.ds(aligned(start, 16), low), cols, "x", (pl.ds(0, low), slice(None))),
+        Cut(pl.ds(aligned(start + low, 16), high), cols, "y", (pl.ds(low, high), slice(None))),
+    )
+
+
+def attend_cuts(core, g):
+    cols = pl.ds(aligned(256 * g + 128 * core, 128), 128)
+    low, high = (16, 32) if g % 2 == 0 else (32, 16)
+    return Cut(pl.ds(0, BLOCK), cols), row_parts(0, low, high, cols)
+
+
+def merge_cuts(core):
+    cols = pl.ds(aligned(384 * core, 128), 384)
+    return Cut(pl.ds(0, BLOCK), cols), row_parts(0, 32, 16, cols)
+
+
+def expand_cuts(core, j):
+    at = PART * j + 256 * core
+    rows = pl.ds(0, BLOCK)
+    whole = Cut(rows, pl.ds(aligned(at, 128), 256))
+    return whole, tuple(
+        Cut(rows, pl.ds(aligned(at + 128 * n, 128), 128), "xy"[n], (slice(None), pl.ds(128 * n, 128))) for n in range(2)
+    )
+
+
+def shrink_cuts(core, j):
+    cols = pl.ds(aligned(384 * core, 128), 384)
+    half = SLICE // 2
+    return Cut(pl.ds(aligned(SLICE * j, SLICE), SLICE), cols), row_parts(SLICE * j, half, half, cols)
+
+
+ALL = slice(None)
+
+
+def blocks(ref, z, y, x, cut):
+    if len(ref.shape) == 6:
+        return ref.at[z, y, x, :, cut.rows, cut.cols]
+    return ref.at[z, y, x, cut.rows, cut.cols]
+
+
+class Gather:
+    def __init__(self, place, ref, cuts, send, recv, twin_send, twin_recv):
+        self.place, self.ref, (self.whole, self.parts) = place, ref, cuts
+        self.send, self.recv, self.twin_send, self.twin_recv = send, recv, twin_send, twin_recv
+
+    def along_z(self, n, part):
+        p = self.place
+        here = blocks(self.ref, p.z, p.y, p.x, part)
+        return [remote(here, here, self.send.at[n, m], self.recv.at[n, m], p.over_z[m]) for m in range(3)]
+
+    def second(self, n, part):
+        p = self.place
+        here = blocks(self.ref, ALL, p.y, p.x, part)
+        return remote(here, here, self.send.at[n, 3], self.recv.at[n, 3], p.over_x if part.first == "x" else p.over_y)
+
+    def third(self, n, part):
+        p = self.place
+        if part.first == "x":
+            here, peer = blocks(self.ref, ALL, p.y, ALL, part), p.over_y
+        else:
+            here, peer = blocks(self.ref, ALL, ALL, p.x, part), p.over_x
+        return remote(here, here, self.send.at[n, 4], self.recv.at[n, 4], peer)
+
+    def to_twin(self):
+        here = blocks(self.ref, ALL, ALL, ALL, self.whole)
+        return remote(here, here, self.twin_send, self.twin_recv, self.place.twin)
+
+    def start_z(self):
+        for n, part in enumerate(self.parts):
+            for copy in self.along_z(n, part):
+                copy.start()
+
+    def start_second(self):
+        for n, part in enumerate(self.parts):
+            for copy in self.along_z(n, part):
+                copy.wait_recv()
+            self.second(n, part).start()
+
+    def start_third(self):
+        for n, part in enumerate(self.parts):
+            self.second(n, part).wait_recv()
+            self.third(n, part).start()
+
+    def start_twin(self):
+        for n, part in enumerate(self.parts):
+            self.third(n, part).wait_recv()
+        self.to_twin().start()
+
+    def ready(self):
+        self.to_twin().wait_recv()
+
+    def finish(self):
+        for n, part in enumerate(self.parts):
+            for copy in self.along_z(n, part):
+                copy.wait_send()
+            self.second(n, part).wait_send()
+            self.third(n, part).wait_send()
+        self.to_twin().wait_send()
+
+VEC_ROWS = 16
+ROW_MERGE, ROW_EXPAND, ROW_SHRINK, ROW_GAIN, ROW_SHIFT = 2, 3, 9, 10, 12
+
+
+def place_vectors(place, pieces_ref, out_ref):
+    pieces = pieces_ref[...].astype(bf16)
+    source = lax.broadcasted_iota(jnp.int32, (LANES, D), 0)
+    target = lax.broadcasted_iota(jnp.int32, (LANES, D), 1)
+
+    def spread(width, offset):
+        chosen = (target == source + offset) & (source < width)
+        return dot_nn(pieces, jnp.where(chosen, 1.0, 0.0).astype(bf16))
+
+    per_row = D // 48
+    attend = spread(48, 48 * (place.index % per_row))
+    single = spread(24, 24 * place.index)
+    expand = spread(SLICE, SLICE * place.chip)
+    out_ref[...] = jnp.zeros((VEC_ROWS, D), f32)
+    half = place.index // per_row
+    out_ref[0:1, :] = jnp.where(half == 0, attend[0:1], 0.0)
+    out_ref[1:2, :] = jnp.where(half == 1, attend[0:1], 0.0)
+    out_ref[2:3, :] = single[1:2]
+    out_ref[3:6, :] = jnp.where(place.c == 0, expand[2:5], 0.0)
+    out_ref[6:9, :] = jnp.where(place.c == 1, expand[2:5], 0.0)
+    out_ref[9:14, :] = single[5:10]
+
+
+def compose(place, pack_ref, twin_ref, target_ref, source_cols, target_cols):
+    half = BLOCK // 2
+    mine = pack_ref[:, source_cols].astype(f32)[:half]
+    other = twin_ref[:, source_cols].astype(f32)[:half]
+    first = jnp.where(place.c == 0, mine, other)
+    second = jnp.where(place.c == 0, other, mine)
+    both = jnp.concatenate([first, second], axis=0).astype(bf16)
+    if len(target_ref.shape) == 6:
+        n = target_cols[0]
+        target_ref[place.z, place.y, place.x, n, :, target_cols[1]] = both
+    else:
+        target_ref[place.z, place.y, place.x, :, target_cols] = both
+
+
+def forward_kernel(
+    bucket, lengths, keeps, x_any, g_any, pack_ref, shrink_ref, pieces_ref,
+    out_any, wa_any, wm_any, we_any, ws_any, qkv_any, mixed_any, logsum_any, xhat_any, rstd_any, lowt_any, xt_any,
+    active_any, slope_any, second_any, vec_out, gain_out,
+    wa, wm, we, ws, pack_twin, vecs, vec_land, x_ref, g_ref, q, k, v, query_const, key_const, keep_table,
+    mixed, logsum, xhat, rstd, low, turned, active, slope, acc, out,
+    send, recv, twin_send, twin_recv, own_send, own_recv, vec_send, vec_recv, local, flow,
+):
+    place = Place()
+    c = place.c
+    x_copy = pltpu.make_async_copy(x_any, x_ref, local.at[0])
+    g_copy = pltpu.make_async_copy(g_any, g_ref, local.at[1])
+    x_copy.start()
+    g_copy.start()
+    place.greet()
+
+    own_pack = remote(pack_ref, pack_twin, own_send.at[0], own_recv.at[0], place.twin)
+    own_pack.start()
+    half = FF_BLOCK // 2
+    their_cols = pl.ds(aligned(384 * (1 - c), 128), 384)
+    my_rows = pl.ds(aligned(half * c, half), half)
+    own_shrink = remote(
+        shrink_ref.at[:, their_cols],
+        ws.at[place.z, place.y, place.x, my_rows, their_cols],
+        own_send.at[1], own_recv.at[1], place.twin,
+    )
+    own_shrink.start()
+    place_vectors(place, pieces_ref, vecs.at[0])
+
+    def vec_copy(step, m, peer):
+        return remote(vecs.at[step], vec_land.at[step + m], vec_send.at[step + m], vec_recv.at[step + m], peer)
+
+    vec_steps = [vec_copy(0, 0, place.twin), vec_copy(1, 0, place.over_x), vec_copy(2, 0, place.over_y)]
+    vec_last = [vec_copy(3, m, place.over_z[m]) for m in range(3)]
+
+    def vec_next(step):
+        vec_steps[step].wait_recv()
+        vecs[step + 1] = vecs[step] + vec_land[step]
+
+    vec_steps[0].start()
+
+    def gather(ref, cuts, at):
+        return Gather(place, ref, cuts, send.at[at], recv.at[at], twin_send.at[at], twin_recv.at[at])
+
+    def job(t):
+        if isinstance(t, int) and t < 3:
+            return [gather(wa, attend_cuts(c, t), t)]
+        if isinstance(t, int) and t == 3:
+            return [gather(wm, merge_cuts(c), 3)]
+        j = t - 4
+        return [
+            gather(we, expand_cuts(c, j), 4 + 2 * j),
+            gather(ws, shrink_cuts(c, j), 5 + 2 * j),
+        ]
+
+    def each(t, action):
+        for one in job(t):
+            getattr(one, action)()
+
+    own_pack.wait_recv()
+    for n in range(3):
+        for g in range(3):
+            cols = aligned(256 * g + 128 * c, 128)
+            compose(place, pack_ref, pack_twin, wa, pl.ds(aligned(D * n + cols, 128), 128), (n, pl.ds(cols, 128)))
+    each(0, "start_z")
+    cols = aligned(384 * c, 128)
+    compose(place, pack_ref, pack_twin, wm, pl.ds(aligned(3 * D + cols, 128), 384), pl.ds(cols, 384))
+    for t in range(1, 4):
+        each(t, "start_z")
+    vec_next(0)
+    vec_steps[1].start()
+    for j in range(JOBS):
+        cols = aligned(PART * j + 256 * c, 128)
+        compose(place, pack_ref, pack_twin, we, pl.ds(aligned(4 * D + cols, 128), 256), pl.ds(cols, 256))
+    my_cols = pl.ds(aligned(384 * c, 128), 384)
+    ws[place.z, place.y, place.x, my_rows, my_cols] = shrink_ref[:, my_cols]
+    own_shrink.wait_recv()
+    for t in range(4, 4 + JOBS):
+        each(t, "start_z")
+    vec_next(1)
+    vec_steps[2].start()
+    each(0, "start_second")
+    token_tables(
+        bucket[0], [lengths[0, b] for b in range(SLOTS)], [keeps[0, b] for b in range(SLOTS)],
+        query_const, key_const, keep_table,
+    )
+    vec_next(2)
+    for copy in vec_last:
+        copy.start()
+    each(1, "start_second")
+    each(0, "start_third")
+    x_copy.wait()
+    turned[...] = x_ref[...].T
+    xt_out = pltpu.make_async_copy(turned, xt_any, flow.at[2, 0])
+    xt_out.start()
+    logsum[...] = jnp.zeros_like(logsum)
+    for copy in vec_last:
+        copy.wait_recv()
+    vec = vecs.at[4]
+    vec[...] = vecs[3] + vec_land[3] + vec_land[4] + vec_land[5]
+
+    def tick(t):
+        each(t, "start_twin")
+        if t + 2 < 4 + JOBS:
+            each(t + 2, "start_second")
+        if t + 1 < 4 + JOBS:
+            each(t + 1, "start_third")
+
+    outgoing = []
+
+    def emit(source, target, n):
+        copy = pltpu.make_async_copy(source, target, local.at[n])
+        copy.start()
+        outgoing.append(copy)
+
+    def project(g):
+        cols = pl.ds(aligned(256 * g, 256), 256)
+        x = x_ref[...]
+        q[:, cols] = ((dot_nn(x, wa[:, :, :, 0, :, cols].reshape(D, 256)) + vec[0:1, cols]) * 0.125).astype(bf16)
+        k[:, cols] = dot_nn(x, wa[:, :, :, 1, :, cols].reshape(D, 256)).astype(bf16)
+        v[:, cols] = (dot_nn(x, wa[:, :, :, 2, :, cols].reshape(D, 256)) + vec[1:2, cols]).astype(bf16)
+
+    tick(0)
+
+    def heads(i, carry):
+        for g in range(3):
+
+            @pl.when(i == 4 * g)
+            def _():
+                each(g, "ready")
+
+        @pl.when(i % 4 == 0)
+        def _():
+            project(i // 4)
+
+        for g in range(3):
+
+            @pl.when(i == 4 * g + 2)
+            def _():
+                tick(g + 1)
+
+        attend_forward(i, query_const, key_const, q, k, v, mixed, logsum, LONG)
+        return carry
+
+    lax.fori_loop(0, 12, heads, 0)
+    emit(wa, wa_any, 2)
+    emit(q, qkv_any.at[0], 3)
+    emit(k, qkv_any.at[1], 4)
+    emit(v, qkv_any.at[2], 5)
+    emit(mixed, mixed_any, 6)
+    emit(logsum, logsum_any, 7)
+
+    tick(4)
+    each(3, "ready")
+    emit(wm, wm_any, 8)
+    first = x_ref[...].astype(f32) + dot_nn(mixed[...], wm[...].reshape(D, D)) + vec[ROW_MERGE : ROW_MERGE + 1, :]
+    x_hat, deviation = norm_parts(first)
+    xhat[...] = x_hat
+    rstd[...] = jnp.broadcast_to(deviation, (TOK_DEV, LANES))
+    normed = x_hat * vec[ROW_GAIN : ROW_GAIN + 1, :] + vec[ROW_SHIFT : ROW_SHIFT + 1, :]
+    low[...] = normed.astype(bf16)
+    acc[...] = normed + vec[ROW_SHRINK : ROW_SHRINK + 1, :]
+    emit(xhat, xhat_any, 9)
+    emit(rstd, rstd_any, 10)
+    xt_out.wait()
+    turned[...] = low[...].T
+    emit(turned, lowt_any, 11)
+
+    def flow_copies(j):
+        return (
+            pltpu.make_async_copy(active.at[j % 2], active_any.at[j], flow.at[0, j % 2]),
+            pltpu.make_async_copy(slope.at[j % 2], slope_any.at[j], flow.at[1, j % 2]),
+        )
+
+    def part(j, carry):
+        @pl.when(j > 0)
+        def _():
+            each(j + 4, "start_twin")
+
+        @pl.when((j > 0) & (j + 2 < JOBS))
+        def _():
+            each(j + 6, "start_second")
+
+        @pl.when((j > 0) & (j + 1 < JOBS))
+        def _():
+            each(j + 5, "start_third")
+
+        @pl.when(j >= 2)
+        def _():
+            for copy in flow_copies(j):
+                copy.wait()
+
+        each(j + 4, "ready")
+        a_ref, s_ref = active.at[j % 2], slope.at[j % 2]
+        for h in range(2):
+            cols = pl.ds(aligned(PART * j + 256 * h, 256), 256)
+            bias = vec[pl.ds(ROW_EXPAND + j, 1), pl.ds(256 * h, 256)]
+            expanded = dot_nn(low[...], we[:, :, :, :, cols].reshape(D, 256)) + bias
+            a, s = gelu_parts(expanded)
+            a_ref[:, 256 * h : 256 * h + 256] = a.astype(bf16)
+            s_ref[:, 256 * h : 256 * h + 256] = s.astype(bf16)
+        rows = pl.ds(aligned(SLICE * j, SLICE), SLICE)
+        acc[...] += dot_nn(a_ref[...], ws[:, :, :, rows, :].reshape(PART, D))
+        for copy in flow_copies(j):
+            copy.start()
+        return carry
+
+    lax.fori_loop(0, JOBS, part, 0)
+    emit(we, we_any, 12)
+    emit(ws, ws_any, 13)
+    g_copy.wait()
+    gain_out[...] = jnp.zeros_like(gain_out)
+    tile = 512
+
+    def last(i, carry):
+        rows = pl.ds(aligned(i * tile, tile), tile)
+        x_hat, deviation = norm_parts(acc[rows, :])
+        gain = vec[ROW_GAIN + 1 : ROW_GAIN + 2, :]
+        result = x_hat * gain + vec[ROW_SHIFT + 1 : ROW_SHIFT + 2, :]
+        keep = jnp.tile(keep_table[rows, :], (1, D // LANES)) > 0.0
+        out[rows, :] = jnp.where(keep, result, x_ref[rows, :].astype(f32)).astype(bf16)
+        dy = jnp.where(keep, g_ref[rows, :].astype(f32), 0.0)
+        grad = norm_back(dy * gain, x_hat, deviation)
+        acc[rows, :] = grad
+        gain_out[ROW_GAIN + 1 : ROW_GAIN + 2, :] += jnp.sum(dy * x_hat, axis=0, keepdims=True)
+        gain_out[ROW_SHIFT + 1 : ROW_SHIFT + 2, :] += jnp.sum(dy, axis=0, keepdims=True)
+        gain_out[ROW_SHRINK : ROW_SHRINK + 1, :] += jnp.sum(grad.astype(bf16).astype(f32), axis=0, keepdims=True)
+        return carry
+
+    lax.fori_loop(0, TOK_DEV // tile, last, 0)
+    emit(acc, second_any, 14)
+    emit(out, out_any, 15)
+    vec_out[...] = vec[...]
+    for j in (JOBS - 2, JOBS - 1):
+        for copy in flow_copies(j):
+            copy.wait()
+    for copy in outgoing:
+        copy.wait()
+    own_pack.wait_send()
+    own_shrink.wait_send()
+    for copy in vec_steps + vec_last:
+        copy.wait_send()
+    for t in range(4):
+        each(t, "finish")
+
+    def finish(j, carry):
+        each(j + 4, "finish")
+        return carry
+
+    lax.fori_loop(0, JOBS, finish, 0)
+
+
+ANY = pl.BlockSpec(memory_space=pl.ANY)
+VM = pl.BlockSpec(memory_space=pltpu.VMEM)
+SM = pl.BlockSpec(memory_space=pltpu.SMEM)
+
+
+def shape(dims, kind):
+    return jax.ShapeDtypeStruct(dims, kind)
+
+
+T = TOK_DEV
+WEIGHTS = (
+    ((Z, Y, X, 3, BLOCK, D), bf16),
+    ((Z, Y, X, BLOCK, D), bf16),
+    ((Z, Y, X, BLOCK, FF), bf16),
+    ((Z, Y, X, FF_BLOCK, D), bf16),
+)
+
+
+def forward_call(buckets, lengths, keeps, inputs, upstream, pack, shrink, pieces):
+    dma = pltpu.SemaphoreType.DMA
+    saved = (
+        ((3, T, D), bf16),
+        ((T, D), bf16),
+        ((T, LANES), f32),
+        ((T, D), f32),
+        ((T, LANES), f32),
+        ((D, T), bf16),
+        ((D, T), bf16),
+        ((JOBS, T, PART), bf16),
+        ((JOBS, T, PART), bf16),
+        ((T, D), f32),
+    )
+    results = (((T, D), bf16),) + WEIGHTS + saved
+    vec = ((VEC_ROWS, D), f32)
+    n_gathers = 4 + 2 * JOBS
+    return pl.pallas_call(
+        forward_kernel,
+        out_shape=tuple(shape(*s) for s in results + (vec, vec)),
+        in_specs=[SM, SM, SM, ANY, ANY, VM, VM, VM],
+        out_specs=[ANY] * len(results) + [VM, VM],
+        scratch_shapes=[pltpu.VMEM(*s) for s in WEIGHTS]
+        + [
+            pltpu.VMEM((32, 3 * D + D + FF), bf16),
+            pltpu.VMEM((5, VEC_ROWS, D), f32),
+            pltpu.VMEM((6, VEC_ROWS, D), f32),
+            pltpu.VMEM((T, D), bf16),
+            pltpu.VMEM((T, D), bf16),
+            pltpu.VMEM((T, D), bf16),
+            pltpu.VMEM((T, D), bf16),
+            pltpu.VMEM((T, D), bf16),
+            pltpu.VMEM((T, LANES), bf16),
+            pltpu.VMEM((T, LANES), bf16),
+            pltpu.VMEM((T, LANES), f32),
+            pltpu.VMEM((T, D), bf16),
+            pltpu.VMEM((T, LANES), f32),
+            pltpu.VMEM((T, D), f32),
+            pltpu.VMEM((T, LANES), f32),
+            pltpu.VMEM((T, D), bf16),
+            pltpu.VMEM((D, T), bf16),
+            pltpu.VMEM((2, T, PART), bf16),
+            pltpu.VMEM((2, T, PART), bf16),
+            pltpu.VMEM((T, D), f32),
+            pltpu.VMEM((T, D), bf16),
+            dma((n_gathers, 2, 5)),
+            dma((n_gathers, 2, 5)),
+            dma((n_gathers,)),
+            dma((n_gathers,)),
+            dma((2,)),
+            dma((2,)),
+            dma((6,)),
+            dma((6,)),
+            dma((20,)),
+            dma((3, 2)),
+        ],
+        compiler_params=pltpu.CompilerParams(collective_id=0, has_side_effects=True, vmem_limit_bytes=VMEM_LIMIT),
+        cost_estimate=pl.CostEstimate(flops=20_000_000_000, bytes_accessed=60_000_000, transcendentals=10_000_000),
+    )(buckets, lengths, keeps, inputs, upstream, pack, shrink, pieces)
+
+
+VMEM_LIMIT = 60 * 2**20
+
+
+def pack_weights(attend, merge, expand):
+    expand = expand.reshape(-1, CHIPS, JOBS, SLICE).transpose(0, 2, 1, 3).reshape(-1, FF)
+    pack = jnp.concatenate([attend, merge, expand], axis=1)
+    return jnp.pad(pack, ((0, 8), (0, 0)))
+
+
+def pack_pieces(attend_bias, merge_bias, expand_bias, shrink_bias, gain, shift):
+    def row(piece):
+        return jnp.pad(piece.astype(f32), ((0, 0), (0, LANES - piece.shape[1])))
+
+    rows = [
+        row(attend_bias[None]), row(merge_bias[None]), row(expand_bias.reshape(3, SLICE)), row(shrink_bias[None]),
+        row(gain), row(shift), jnp.zeros((6, LANES), f32),
+    ]
+    return jnp.concatenate(rows, axis=0)
+
+class Reduce:
+    def __init__(self, place, ref, lands, final, cuts, twin_cuts, sems):
+        self.place, self.ref, (self.whole, self.parts), self.twin_whole = place, ref, cuts, twin_cuts[0]
+        self.lands, self.final = lands, final
+        self.send, self.recv, self.twin_send, self.twin_recv = sems
+        self.deep = len(ref.shape) == 6
+
+    def land(self, step, n, part, m=None):
+        rows, cols = part.near
+        ref = self.lands[step]
+        index = () if m is None else (m,)
+        lead = len(ref.shape) - 2 - len(index)
+        return ref.at[index + (ALL,) * lead + (rows, cols)]
+
+    def sent(self, n, part, step):
+        p = self.place
+        if part.first == "x":
+            return blocks(self.ref, ALL, ALL, 1 - p.x, part) if step == 1 else blocks(self.ref, ALL, 1 - p.y, p.x, part)
+        return blocks(self.ref, ALL, 1 - p.y, ALL, part) if step == 1 else blocks(self.ref, ALL, p.y, 1 - p.x, part)
+
+    def kept(self, n, part, step):
+        p = self.place
+        if part.first == "x":
+            return blocks(self.ref, ALL, ALL, p.x, part) if step == 1 else blocks(self.ref, ALL, p.y, p.x, part)
+        return blocks(self.ref, ALL, p.y, ALL, part) if step == 1 else blocks(self.ref, ALL, p.y, p.x, part)
+
+    def twin(self):
+        source = blocks(self.ref, ALL, ALL, ALL, self.twin_whole)
+        return remote(source, self.lands[0], self.twin_send, self.twin_recv, self.place.twin)
+
+    def stage(self, n, part, step):
+        p = self.place
+        peer = p.over_x if (part.first == "x") == (step == 1) else p.over_y
+        return remote(
+            self.sent(n, part, step), self.land(step, n, part), self.send.at[n, step - 1], self.recv.at[n, step - 1], peer
+        )
+
+    def along_z(self, n, part):
+        p = self.place
+        return [
+            remote(
+                blocks(self.ref, p.other_z[m], p.y, p.x, part), self.land(3, n, part, m),
+                self.send.at[n, 2 + m], self.recv.at[n, 2 + m], p.over_z[m],
+            )
+            for m in range(3)
+        ]
+
+    def start_twin(self):
+        self.twin().start()
+
+    def start_first(self):
+        self.twin().wait_recv()
+        mine = blocks(self.ref, ALL, ALL, ALL, self.whole)
+        mine[...] = (mine[...].astype(f32) + self.lands[0][...].astype(f32)).astype(bf16)
+        for n, part in enumerate(self.parts):
+            self.stage(n, part, 1).start()
+
+    def add(self, n, part, step):
+        self.stage(n, part, step).wait_recv()
+        mine, other = self.kept(n, part, step), self.land(step, n, part)
+        mine[...] = (mine[...].astype(f32) + other[...].astype(f32)).astype(bf16)
+
+    def start_second(self):
+        for n, part in enumerate(self.parts):
+            self.add(n, part, 1)
+            self.stage(n, part, 2).start()
+
+    def start_z(self):
+        for n, part in enumerate(self.parts):
+            self.add(n, part, 2)
+            for copy in self.along_z(n, part):
+                copy.start()
+
+    def total(self):
+        p = self.place
+        for n, part in enumerate(self.parts):
+            for copy in self.along_z(n, part):
+                copy.wait_recv()
+            value = blocks(self.ref, p.z, p.y, p.x, part)[...].astype(f32)
+            for m in range(3):
+                value += self.land(3, n, part, m)[...].astype(f32)
+            index = (ALL,) if self.deep else ()
+            self.final[index + (part.rows, part.cols)] = value
+
+    def finish(self):
+        self.twin().wait_send()
+        for n, part in enumerate(self.parts):
+            for step in (1, 2):
+                self.stage(n, part, step).wait_send()
+            for copy in self.along_z(n, part):
+                copy.wait_send()
+
+
+def backward_kernel(
+    bucket, lengths, keeps, wa_any, wm_any, we_any, ws_any, qkv_any, mixed_any, logsum_any, xhat_any, rstd_any,
+    lowt_any, xt_any, active_any, slope_any, second_any, g_any, vec, gain_in,
+    ig_any, ga_out, gm_out, ge_out, gs_out, vec_out,
+    wa, wm, we, ws, ga,
+    a0, a1, a2, a3, m0, m1, m2, m3, e0, e1, e2, e3, s0, s1, s2, s3, fa, fm, fe, fs,
+    q, k, v, query_const, key_const, keep_table, mixed, logsum, xhat, rstd, turned, low_grad, active, slope, first,
+    mixed_grad, gain, vec_land,
+    send, recv, twin_send, twin_recv, last_send, last_recv, vec_send, vec_recv, local, flow,
+):
+    place = Place()
+    c = place.c
+
+    def load(source, target, n):
+        copy = pltpu.make_async_copy(source, target, local.at[n])
+        copy.start()
+        return copy
+
+    def flow_copies(j):
+        return (
+            pltpu.make_async_copy(active_any.at[j], active.at[j % 2], flow.at[0, j % 2]),
+            pltpu.make_async_copy(slope_any.at[j], slope.at[j % 2], flow.at[1, j % 2]),
+        )
+
+    in_second = load(second_any, first, 0)
+    in_ws = load(ws_any, ws, 1)
+    for copy in flow_copies(0):
+        copy.start()
+    in_we = load(we_any, we, 2)
+    in_lowt = load(lowt_any, turned, 3)
+    later = [
+        load(xhat_any, xhat, 4), load(rstd_any, rstd, 5), load(wm_any, wm, 6), load(mixed_any, mixed, 7),
+        load(logsum_any, logsum, 8), load(qkv_any.at[0], q, 9), load(qkv_any.at[1], k, 10), load(qkv_any.at[2], v, 11),
+        load(wa_any, wa, 12),
+    ]
+    place.greet()
+    token_tables(
+        bucket[0], [lengths[0, b] for b in range(SLOTS)], [keeps[0, b] for b in range(SLOTS)],
+        query_const, key_const, keep_table,
+    )
+    gain[0] = gain_in[...]
+
+    def reduction(ref, lands, final, cuts, at, *args):
+        sems = (send.at[at], recv.at[at], twin_send.at[at], twin_recv.at[at])
+        return Reduce(place, ref, lands, final, cuts(c, *args), cuts(1 - c, *args), sems)
+
+    def job(t):
+        if t < JOBS:
+            return [
+                reduction(we, [e0.at[t % 2]] + [r.at[t] for r in (e1, e2, e3)], fe, expand_cuts, 2 * t, t),
+                reduction(ws, [s0.at[t % 2]] + [r.at[t] for r in (s1, s2, s3)], fs, shrink_cuts, 2 * t + 1, t),
+            ]
+        if t == JOBS:
+            return [reduction(wm, [m0, m1, m2, m3], fm, merge_cuts, 2 * JOBS)]
+        g = t - JOBS - 1
+        return [reduction(ga, [r.at[g] for r in (a0, a1, a2, a3)], fa, attend_cuts, 2 * JOBS + 1 + g, g)]
+
+    ACTIONS = {0: "start_twin", 1: "start_first", 2: "start_second", 3: "start_z", 4: "total"}
+
+    def events(names):
+        for step, t in names:
+            for one in job(t):
+                getattr(one, ACTIONS[step])()
+
+    def when(index, table):
+        for value, names in table.items():
+
+            @pl.when(index == value)
+            def _():
+                events(names)
+
+    in_second.wait()
+    low_grad[...] = first[...].astype(bf16)
+    in_ws.wait()
+    in_we.wait()
+    in_lowt.wait()
+
+    def part(j, carry):
+        for copy in flow_copies(j):
+            copy.wait()
+
+        @pl.when(j + 1 < JOBS)
+        def _():
+            for copy in flow_copies(j + 1):
+                copy.start()
+
+        a_ref, s_ref = active.at[j % 2], slope.at[j % 2]
+        rows = pl.ds(aligned(SLICE * j, SLICE), SLICE)
+        cols = pl.ds(aligned(PART * j, PART), PART)
+        s_in = low_grad[...]
+        for h in range(2):
+            here = slice(256 * h, 256 * h + 256)
+            e_in = dot_nt(s_in, ws[2 * h : 2 * h + 2, :, :, rows, :].reshape(256, D)) * s_ref[:, here].astype(f32)
+            e_in = e_in.astype(bf16)
+            s_ref[:, here] = e_in
+            gain[0, pl.ds(ROW_EXPAND + j, 1), here] = jnp.sum(e_in.astype(f32), axis=0, keepdims=True)
+        when(j, FFN_MIDDLE)
+        for h in range(2):
+            here = slice(256 * h, 256 * h + 256)
+            grad = dot_tn(a_ref[:, here], s_in).astype(bf16)
+            ws[2 * h : 2 * h + 2, :, :, rows, :] = grad.reshape(2, Y, X, SLICE, D)
+        e_in = s_ref[...]
+        first[...] += dot_nt(e_in, we[:, :, :, :, cols].reshape(D, PART))
+        for h in range(2):
+            here = pl.ds(aligned(PART * j + 256 * h, 256), 256)
+            grad = dot_nn(turned[...], s_ref[:, 256 * h : 256 * h + 256]).astype(bf16)
+            we[:, :, :, :, here] = grad.reshape(Z, Y, X, BLOCK, 256)
+        when(j, {t: [(0, t)] for t in range(JOBS)})
+        return carry
+
+    lax.fori_loop(0, JOBS, part, 0)
+    in_xt = load(xt_any, turned, 13)
+    events(AFTER_FFN)
+    for copy in later[:4]:
+        copy.wait()
+    for row in (ROW_MERGE, ROW_GAIN, ROW_SHIFT):
+        gain[0, row : row + 1, :] = jnp.zeros((1, D), f32)
+    tile = 512
+
+    def middle(i, carry):
+        rows = pl.ds(aligned(i * tile, tile), tile)
+        dy, x_hat = first[rows, :], xhat[rows, :]
+        deviation = jnp.tile(rstd[rows, :], (1, D // LANES))
+        grad = norm_back(dy * vec[ROW_GAIN : ROW_GAIN + 1, :], x_hat, deviation)
+        first[rows, :] = grad
+        branch = grad.astype(bf16)
+        low_grad[rows, :] = branch
+        gain[0, ROW_GAIN : ROW_GAIN + 1, :] += jnp.sum(dy * x_hat, axis=0, keepdims=True)
+        gain[0, ROW_SHIFT : ROW_SHIFT + 1, :] += jnp.sum(dy, axis=0, keepdims=True)
+        gain[0, ROW_MERGE : ROW_MERGE + 1, :] += jnp.sum(branch.astype(f32), axis=0, keepdims=True)
+        mixed_grad[rows, :] = dot_nt(branch, wm[...].reshape(D, D)).astype(bf16)
+        return carry
+
+    lax.fori_loop(0, TOK_DEV // tile, middle, 0)
+    events(AFTER_NORM)
+    wm[...] = dot_tn(mixed[...], low_grad[...]).astype(bf16).reshape(Z, Y, X, BLOCK, D)
+    events([(0, JOBS)])
+    for copy in later[4:]:
+        copy.wait()
+    in_xt.wait()
+
+    def heads(i, carry):
+        when(i, HEADS_BEFORE)
+        attend_backward(i, query_const, key_const, q, k, v, mixed, logsum, mixed_grad, q, k, v, LONG)
+
+        @pl.when(i % 4 == 3)
+        def _():
+            cols = pl.ds(aligned(256 * (i // 4), 256), 256)
+            for n, grads in enumerate((q, k, v)):
+                grad = dot_nn(turned[...], grads[:, cols]).astype(bf16)
+                ga[:, :, :, n, :, cols] = grad.reshape(Z, Y, X, BLOCK, 256)
+                if n != 1:
+                    gain[0, n // 2 : n // 2 + 1, cols] = jnp.sum(grads[:, cols].astype(f32), axis=0, keepdims=True)
+
+        when(i, {4 * g + 3: [(0, JOBS + 1 + g)] for g in range(3)})
+        return carry
+
+    lax.fori_loop(0, 12, heads, 0)
+
+    def vec_copy(step, m, peer):
+        return remote(gain.at[step], vec_land.at[step + m], vec_send.at[step + m], vec_recv.at[step + m], peer)
+
+    vec_steps = [vec_copy(0, 0, place.twin), vec_copy(1, 0, place.over_x), vec_copy(2, 0, place.over_y)]
+    vec_last = [vec_copy(3, m, place.over_z[m]) for m in range(3)]
+    vec_steps[0].start()
+    in_g = load(g_any, mixed, 14)
+
+    half, ff_half = BLOCK // 2, FF_BLOCK // 2
+
+    def last_copy(ref, n, cols, height):
+        rows = pl.ds(aligned(height * (1 - c), 8), height)
+        here = ref.at[:, rows, cols] if len(ref.shape) == 3 else ref.at[rows, cols]
+        return remote(here, here, last_send.at[n], last_recv.at[n], place.twin)
+
+    early_last = [last_copy(fm, 0, merge_cuts(c)[0].cols, half), last_copy(fs, 1, merge_cuts(c)[0].cols, ff_half)]
+    early_last += [last_copy(fe, 2 + j, expand_cuts(c, j)[0].cols, half) for j in range(JOBS)]
+    attend_last = [last_copy(fa, 2 + JOBS + g, attend_cuts(c, g)[0].cols, half) for g in range(3)]
+
+    events(TAIL[0])
+    vec_steps[0].wait_recv()
+    gain[1] = gain[0] + vec_land[0]
+    vec_steps[1].start()
+    for copy in early_last:
+        copy.start()
+    in_g.wait()
+
+    def inputs_part(i, carry):
+        rows = pl.ds(aligned(i * tile, tile), tile)
+        keep = jnp.tile(keep_table[rows, :], (1, D // LANES)) > 0.0
+        total = first[rows, :] + jnp.where(keep, 0.0, mixed[rows, :].astype(f32))
+        for n, grads in enumerate((q, k, v)):
+            total += dot_nt(grads[rows, :], wa[:, :, :, n, :, :].reshape(D, D))
+        first[rows, :] = total
+
+        @pl.when(i == 0)
+        def _():
+            events(TAIL[1])
+            vec_steps[1].wait_recv()
+            gain[2] = gain[1] + vec_land[1]
+            vec_steps[2].start()
+
+        return carry
+
+    lax.fori_loop(0, TOK_DEV // tile, inputs_part, 0)
+    out_ig = pltpu.make_async_copy(first, ig_any, local.at[15])
+    out_ig.start()
+    events(TAIL[2])
+    vec_steps[2].wait_recv()
+    gain[3] = gain[2] + vec_land[2]
+    for copy in vec_last:
+        copy.start()
+    attend_last[0].start()
+    attend_last[1].start()
+    for copy in early_last:
+        copy.wait_recv()
+    mine, ff_mine = pl.ds(aligned(half * c, 8), half), pl.ds(aligned(ff_half * c, 8), ff_half)
+    gm_out[...] = fm[mine, :]
+    ge_out[...] = fe[mine, :]
+    gs_out[...] = fs[ff_mine, :]
+    events(TAIL[3])
+    attend_last[2].start()
+    for copy in vec_last:
+        copy.wait_recv()
+    vec_out[...] = gain[3] + vec_land[3] + vec_land[4] + vec_land[5]
+    for copy in early_last:
+        copy.wait_send()
+    for copy in vec_steps + vec_last:
+        copy.wait_send()
+    for t in range(JOBS + 4):
+        for one in job(t):
+            one.finish()
+    for copy in attend_last:
+        copy.wait_recv()
+        copy.wait_send()
+    for n in range(3):
+        ga_out[:, D * n : D * n + D] = fa[n, mine, :]
+    out_ig.wait()
+
+
+FFN_MIDDLE = {
+    1: [(1, 0)],
+    2: [(1, 1)],
+    3: [(2, 0), (1, 2)],
+    4: [(2, 1), (1, 3)],
+    5: [(1, 4)],
+}
+AFTER_FFN = [(3, 0), (2, 2)]
+AFTER_NORM = [(1, 5), (3, 1)]
+HEADS_BEFORE = {
+    0: [(2, 3)],
+    1: [(1, 6), (4, 0)],
+    2: [(3, 2), (4, 1)],
+    3: [(2, 4)],
+    4: [(3, 3), (4, 2)],
+    5: [(2, 5), (1, 7)],
+    6: [(3, 4)],
+    7: [(2, 6), (4, 3)],
+    8: [(3, 5)],
+    9: [(1, 8), (4, 4)],
+    10: [(2, 7), (3, 6)],
+    11: [(4, 5)],
+}
+TAIL = [
+    [(1, 9), (3, 7), (2, 8), (4, 6)],
+    [(2, 9), (3, 8), (4, 7)],
+    [(3, 9), (4, 8)],
+    [(4, 9)],
+]
+
+
+def backward_call(buckets, lengths, keeps, weights, saved, upstream, vec, gain):
+    dma = pltpu.SemaphoreType.DMA
+
+    def landing(jobs, rows, cols, deep=(), slots=None):
+        lead = (jobs,) if jobs else ()
+        return [
+            pltpu.VMEM(((slots,) if slots else lead) + (Z, Y, X) + deep + (rows, cols), bf16),
+            pltpu.VMEM(lead + (Z, 2) + deep + (rows, cols), bf16),
+            pltpu.VMEM(lead + (Z,) + deep + (rows, cols), bf16),
+            pltpu.VMEM(lead + (3,) + deep + (rows, cols), bf16),
+        ]
+
+    n_sums = 4 + 2 * JOBS
+    half, ff_half = BLOCK // 2, FF_BLOCK // 2
+    return pl.pallas_call(
+        backward_kernel,
+        out_shape=(
+            shape((T, D), f32), shape((half, 3 * D), f32), shape((half, D), f32), shape((half, FF), f32),
+            shape((ff_half, D), f32), shape((VEC_ROWS, D), f32),
+        ),
+        in_specs=[SM, SM, SM] + [ANY] * 15 + [VM, VM],
+        out_specs=[ANY] + [VM] * 5,
+        scratch_shapes=[pltpu.VMEM(*s) for s in WEIGHTS]
+        + [pltpu.VMEM(*WEIGHTS[0])]
+        + landing(3, BLOCK, 128, (3,))
+        + landing(0, BLOCK, 384)
+        + landing(JOBS, BLOCK, 256, slots=2)
+        + landing(JOBS, SLICE, 384, slots=2)
+        + [
+            pltpu.VMEM((3, BLOCK, D), f32),
+            pltpu.VMEM((BLOCK, D), f32),
+            pltpu.VMEM((BLOCK, FF), f32),
+            pltpu.VMEM((FF_BLOCK, D), f32),
+            pltpu.VMEM((T, D), bf16),
+            pltpu.VMEM((T, D), bf16),
+            pltpu.VMEM((T, D), bf16),
+            pltpu.VMEM((T, LANES), bf16),
+            pltpu.VMEM((T, LANES), bf16),
+            pltpu.VMEM((T, LANES), f32),
+            pltpu.VMEM((T, D), bf16),
+            pltpu.VMEM((T, LANES), f32),
+            pltpu.VMEM((T, D), f32),
+            pltpu.VMEM((T, LANES), f32),
+            pltpu.VMEM((D, T), bf16),
+            pltpu.VMEM((T, D), bf16),
+            pltpu.VMEM((2, T, PART), bf16),
+            pltpu.VMEM((2, T, PART), bf16),
+            pltpu.VMEM((T, D), f32),
+            pltpu.VMEM((T, D), bf16),
+            pltpu.VMEM((4, VEC_ROWS, D), f32),
+            pltpu.VMEM((6, VEC_ROWS, D), f32),
+            dma((n_sums, 2, 5)),
+            dma((n_sums, 2, 5)),
+            dma((n_sums,)),
+            dma((n_sums,)),
+            dma((5 + JOBS,)),
+            dma((5 + JOBS,)),
+            dma((6,)),
+            dma((6,)),
+            dma((16,)),
+            dma((2, 2)),
+        ],
+        compiler_params=pltpu.CompilerParams(collective_id=1, has_side_effects=True, vmem_limit_bytes=VMEM_LIMIT),
+        cost_estimate=pl.CostEstimate(flops=40_000_000_000, bytes_accessed=60_000_000, transcendentals=10_000_000),
+    )(buckets, lengths, keeps, *weights, *saved, upstream, vec, gain)
 
 def layer_norm(hidden, gains, shifts):
     center = hidden - jnp.mean(hidden, axis=-1, keepdims=True)
@@ -241,7 +1358,7 @@
     return (grads, input_grad)
 
 
-def on_device(
+def general_device(
     inputs,
     upstream,
     buckets,
@@ -314,8 +1431,44 @@
         shares[9],
     )
 
+def slice_device(
+    inputs, upstream, buckets, lengths, layer_keep, attend_weight, attend_bias, merge_weight, merge_bias,
+    expand_weight, expand_bias, shrink_weight, shrink_bias, norm_gain, norm_shift,
+):
+    pack = pack_weights(attend_weight, merge_weight, expand_weight)
+    pieces = pack_pieces(attend_bias, merge_bias, expand_bias, shrink_bias, norm_gain, norm_shift)
+    results = forward_call(buckets, lengths, layer_keep, inputs, upstream, pack, shrink_weight, pieces)
+    outputs, weights, saved, vec, gain = results[0], results[1:5], results[5:-2], results[-2], results[-1]
+    input_grad, attend, merge, expand, shrink, sums = backward_call(
+        buckets, lengths, layer_keep, weights, saved, upstream, vec, gain
+    )
+    expand = expand.reshape(-1, JOBS, CHIPS, SLICE).transpose(0, 2, 1, 3).reshape(-1, FF)
+    group, inner = lax.axis_index("group"), lax.axis_index("inner")
+    index = group * (2 * X) + inner
+    chip, core = index // 2, index % 2
+    width = D // (2 * CHIPS)
+    at = width * index
+
+    def cut(rows, count):
+        return lax.dynamic_slice(sums, (rows, at), (count, width))
+
+    return (
+        outputs,
+        input_grad,
+        attend,
+        lax.dynamic_slice(sums[:2].reshape(-1), (2 * at,), (2 * width,)),
+        merge,
+        cut(ROW_MERGE, 1)[0],
+        expand,
+        lax.dynamic_slice(sums, (ROW_EXPAND + 3 * core, SLICE * chip), (3, SLICE)).reshape(-1),
+        shrink,
+        cut(ROW_SHRINK, 1)[0],
+        cut(ROW_GAIN, 2),
+        cut(ROW_SHIFT, 2),
+    )
 
 def solution(mesh):
+    on_slice = mesh.shape["group"] == Z * Y and mesh.shape["inner"] == 2 * X
     placed = (
         P(("group", "inner"), None),
         P(("group", "inner"), None),
@@ -334,7 +1487,7 @@
         P(None, ("group", "inner")),
     )
     return jax.shard_map(
-        on_device,
+        slice_device if on_slice else general_device,
         mesh=mesh,
         in_specs=placed,
         out_specs=(

time: 848 us -> 253 us (0.30); the launches traced: 839 us -> 253 us
  waiting for transfers between devices: 372 us -> 0 us
  Pallas kernels: 0 us -> 231 us
  matrix products: 175 us -> 0 us
  blocking collectives: 159 us -> 0 us
  local copies, waits for them, and re-layouts: 73.7 us -> 18.5 us
  other arithmetic: 42.4 us -> 1.72 us
  between operations: 15.8 us -> 1.51 us
    reduce_scatter x3 -> x0, waiting for transfers between devices: 284 us -> none  [the longest x1 142 us: on_device(): lax.psum_scatter(grads[6], ('group', 'inner'), scatter_dimension=0, tiled...]
    pallas_call x0 -> x2, Pallas kernels: none -> 231 us  [the longest x1 128 us: forward_call(): pl.pallas_call(forward_kernel, out_shape=tuple((shape(*s) for s in result...]
    dot_general x26 -> x0, matrix products: 175 us -> none  [the longest x4 57.6 us: matmul(): return jnp.dot(left, right, preferred_element_type=jnp.float32)]
    unnamed x2 -> x0, blocking collectives: 82.8 us -> none
    all_gather x2 -> x0, blocking collectives: 76.4 us -> none  [the longest x1 40 us: on_device(): lax.all_gather(norm_gain, ('group', 'inner'), axis=1, tiled=True)]
    unnamed x9 -> x0, waiting for transfers between devices: 65.2 us -> none
    unnamed x129 -> x25, local copies, waits for them, and re-layouts: 35.4 us -> 6.39 us
    all_gather x4 -> x0, waiting for transfers between devices: 23 us -> none  [the longest x1 22.9 us: on_device(): lax.all_gather(shrink_weight, ('group', 'inner'), axis=0, tiled=True)]
  transfers between devices with their start and end apart: 8 -> 0, of which waited for: 4 -> 0; matrix products, arithmetic and copies ran while one was open for 26% -> 0% of each run, Pallas kernels for 0% -> 0%
where the time goes in v1:
time: 253 us
  Pallas kernels  231 us (91%)
  local copies, waits for them, and re-layouts  18.5 us (7%)
    pallas_call x1, Pallas kernels, forward_call(): pl.pallas_call(forward_kernel, out_shape=tuple((shape(*s) for s in result...  128 us
    pallas_call x1, Pallas kernels, backward_call(): pl.pallas_call(backward_kernel, out_shape=(shape((T, D), f32), shape((hal...  103 us
    unnamed x25, local copies, waits for them, and re-layouts  6.39 us

profile of v1, /device:TPU:0, one launch (start us, length us, event | category | flops | bytes accessed | tf_op | source)
XLA Modules:
  0.0 253.0 jit_solution(3147097155069191615)
XLA Ops:
  0.6 0.0 copy-start.8
  0.7 0.0 copy-start.4
  0.7 0.0 copy-start.5
  0.7 0.0 copy-start.9
  0.7 0.0 copy-start.6
  0.7 0.0 copy-start.7
  1.4 1.5 reshape.51
  2.9 0.1 copy.29
  3.0 0.6 reshape.52
  3.6 1.7 fusion.4.pack_ref
  5.3 0.0 copy-done.8
  5.3 0.0 copy-done.4
  5.3 0.0 copy-done.5
  5.4 0.0 copy-done.9
  5.4 0.1 convert_element_type.32
  5.5 0.0 copy-done.6
  5.5 0.0 copy-done.7
  5.5 1.2 concatenate.7.pieces_ref
  6.7 128.0 %shard_map.238 = (bf16[1024,768]{1,0:T(8,128)(2,1)}, bf16[4,2,2,3,48,768]{5,4,3,2,1,0:T(8,128)(2,1)}, bf16[4,2,2,48,768]{4,3,2,1,0:T(8,128)(2,1)}, bf16[4,2,2,48...) custom-call(s32[1]{0:T(128)S(6)} %copy.38.bucket, ...), custom_call_target="tpu_custom_call" | custom-call | flops 20000000000 | bytes 60000000 | tf_op jit(solution)/shard_map/pallas_call | solution.py:643
  134.7 103.3 %shard_map.239 = (f32[1024,768]{1,0:T(8,128)}, f32[24,2304]{1,0:T(8,128)}, f32[24,768]{1,0:T(8,128)}, f32[24,3072]{1,0:T(8,128)}, f32[96,768]{1,0:T(8,128)}, /*index=5*/f32[16,768]{1,0:T(8,128)}) custom-call(s32[1]{0:T(128)S(6)} %copy.38.bucket, s32[1,8]{1,0:T(1,128)} %lengths.3, s32[1,8]{1,0:T(1,128)} %keeps.3, ...), custom_call_target="tpu_custom_call" | custom-call | flops 40000000000 | bytes 60000000 | tf_op jit(solution)/shard_map/pallas_call | solution.py:1083
  238.1 0.7 slice.3
  238.8 0.6 dynamic_slice.18
  239.4 1.3 dynamic-slice_bitcast_fusion
  240.7 1.3 reshape.54
  242.1 0.4 copy.32
  242.5 1.3 reshape.55
  243.7 0.0 copy-start
  243.8 0.9 dynamic_slice.20
  244.7 0.6 reshape.56
  245.3 1.4 constant_dynamic-slice_fusion
  246.7 2.7 %copy.39 = bf16[1024,768]{1,0:T(8,128)(2,1)} copy(bf16[1024,768]{1,0:T(8,128)(2,1)} %get-tuple-element.78) | data formatting | bytes 3145728
  249.3 0.0 copy-done
  249.3 0.0 copy-start.2
  249.3 0.0 copy-start.3
  249.3 0.0 copy-start.1
  249.3 1.7 copy.40
  251.0 0.0 copy-done.2
  251.0 0.7 copy.41
  251.7 0.0 copy-done.3
  251.7 0.6 copy.42
  252.3 0.0 copy-done.1
  252.3 0.7 copy.43
  (6 shorter events, 0.0 us)
Async XLA Ops:
  0.6 4.7 %copy-start.8 = (bf16[48]{0:T(256)(128)(2,1)S(1)}, bf16[48]{0:T(256)(128)(2,1)}, u32[]{:S(2)}) copy-start(bf16[48]{0:T(256)(128)(2,1)} %param.21) | copy-start | bytes 292
  0.7 4.7 %copy-start.4 = (bf16[24]{0:T(256)(128)(2,1)S(1)}, bf16[24]{0:T(256)(128)(2,1)}, u32[]{:S(2)}) copy-start(bf16[24]{0:T(256)(128)(2,1)} %param.27) | copy-start | bytes 148
  0.7 4.7 %copy-start.5 = (bf16[24]{0:T(256)(128)(2,1)S(1)}, bf16[24]{0:T(256)(128)(2,1)}, u32[]{:S(2)}) copy-start(bf16[24]{0:T(256)(128)(2,1)} %param.23) | copy-start | bytes 148
  0.7 4.7 %copy-start.9 = (bf16[96]{0:T(256)(128)(2,1)S(1)}, bf16[96]{0:T(256)(128)(2,1)}, u32[]{:S(2)}) copy-start(bf16[96]{0:T(256)(128)(2,1)} %param.25) | copy-start | bytes 580
  0.7 4.8 %copy-start.6 = (bf16[2,24]{1,0:T(2,128)(2,1)S(1)}, bf16[2,24]{1,0:T(2,128)(2,1)}, u32[]{:S(2)}) copy-start(bf16[2,24]{1,0:T(2,128)(2,1)} %param.29) | copy-start | bytes 292
  0.7 4.8 %copy-start.7 = (bf16[2,24]{1,0:T(2,128)(2,1)S(1)}, bf16[2,24]{1,0:T(2,128)(2,1)}, u32[]{:S(2)}) copy-start(bf16[2,24]{1,0:T(2,128)(2,1)} %param.28) | copy-start | bytes 292
  243.7 5.6 %copy-start = (f32[1024,768]{1,0:T(8,128)S(1)}, f32[1024,768]{1,0:T(8,128)}, u32[]{:S(2)}) copy-start(f32[1024,768]{1,0:T(8,128)} %get-tuple-element.79) | copy-start | bytes 9437188
  249.3 1.7 copy-start.2
  249.3 2.4 copy-start.3
  249.3 3.0 %copy-start.1 = (f32[96,768]{1,0:T(8,128)S(1)}, f32[96,768]{1,0:T(8,128)}, u32[]{:S(2)}) copy-start(f32[96,768]{1,0:T(8,128)} %get-tuple-element.86) | copy-start | bytes 884740

commit v2 on v0

--- a/solution.py
+++ b/solution.py
@@ -1,6 +1,8 @@
 import jax
 import jax.numpy as jnp
 from jax import lax
+from jax.experimental import pallas as pl
+from jax.experimental.pallas import tpu as pltpu
 from jax.sharding import PartitionSpec as P
 
 HEADS = 12
@@ -9,11 +11,1062 @@
 SHORT = 128
 TOK_DEV = 1024
 SLOTS = 8
-
-
+D = 768
+FF = 3072
+LANES = 128
+RSTD_LANE, KEEP_LANE = 12, 13
 epsilon = 1e-05
 masked_score = -1e30
-
+f32 = jnp.float32
+bf16 = jnp.bfloat16
+
+
+def dot_nn(a, b):
+    return lax.dot_general(a, b, (((1,), (0,)), ((), ())), preferred_element_type=f32)
+
+
+def dot_nt(a, b):
+    return lax.dot_general(a, b, (((1,), (1,)), ((), ())), preferred_element_type=f32)
+
+
+def dot_tn(a, b):
+    return lax.dot_general(a, b, (((0,), (0,)), ((), ())), preferred_element_type=f32)
+
+
+def lane_index(rows):
+    return lax.broadcasted_iota(jnp.int32, (rows, LANES), 1)
+
+
+def token_tables(bucket, lengths, keeps, query_const, key_const, columns):
+    shape = (TOK_DEV, LANES)
+    position = lax.broadcasted_iota(jnp.int32, shape, 0)
+    is_long = jnp.broadcast_to(bucket, shape) > 0
+    slot = jnp.where(is_long, (position >> 9) << 2, position >> 7)
+    offset = jnp.where(is_long, position & (LONG - 1), position & (SHORT - 1))
+    length = jnp.zeros(shape, jnp.int32)
+    keep = jnp.zeros(shape, jnp.int32)
+    for b in range(SLOTS):
+        here = slot == b
+        length = jnp.where(here, lengths[b], length)
+        keep = jnp.where(here, keeps[b], keep)
+    length = length + bucket * (LONG - SHORT)
+    valid = offset < length
+    within = jnp.where(is_long, 0, (position >> 7) & 3)
+    lane = lax.broadcasted_iota(jnp.int32, shape, 1) & (HD - 1)
+    is_span = (lane >= 4) & (lane < 8)
+    same = lane - 4 == within
+    zero, one = jnp.zeros(shape, f32), jnp.ones(shape, f32)
+    query_const[...] = jnp.where(lane == 3, one, jnp.where(is_span & ~same, one, zero)).astype(bf16)
+    key_const[...] = jnp.where(
+        lane < 3,
+        one,
+        jnp.where(((lane == 3) & ~valid) | (is_span & same), masked_score * one, zero),
+    ).astype(bf16)
+    columns[...] = jnp.where((lane_index(TOK_DEV) == KEEP_LANE) & (keep > 0), one, zero)
+
+
+def column_of(columns, lane):
+    return jnp.sum(jnp.where(lane_index(columns.shape[0]) == lane, columns, 0.0), axis=1, keepdims=True)
+
+
+def three_parts(column, rows):
+    wide = jnp.broadcast_to(column, (rows, LANES))
+    high = wide.astype(bf16)
+    rest = wide - high.astype(f32)
+    middle = rest.astype(bf16)
+    low = (rest - middle.astype(f32)).astype(bf16)
+    return high, middle, low
+
+
+def attend_forward(index, query_const, key_const, q_ref, k_ref, v_ref, mixed_ref, logsum_ref, tile):
+    pair, block = index // 2, index % 2
+    cols = pl.ds(pl.multiple_of(pair * LANES, LANES), LANES)
+    rows = pl.ds(pl.multiple_of(block * LONG, LONG), LONG)
+    lane_k = lane_index(LONG)
+    k2, v2 = k_ref[rows, cols], v_ref[rows, cols]
+    kc = key_const[rows, :]
+    k_aug = [jnp.where((lane_k // HD) == half, k2, kc) for half in range(2)]
+    lane_q = lane_index(tile)
+    for t in range(LONG // tile):
+        qrows = pl.ds(pl.multiple_of(block * LONG + t * tile, tile), tile)
+        q2, qc = q_ref[qrows, cols], query_const[qrows, :]
+        outs = []
+        sums = logsum_ref[qrows, :]
+        for half in range(2):
+            q_aug = jnp.where((lane_q // HD) == half, q2, qc)
+            scores = dot_nt(q_aug, k_aug[half])
+            highest = jnp.max(scores, axis=1, keepdims=True)
+            raised = jnp.exp(scores - highest)
+            total = jnp.sum(raised, axis=1, keepdims=True)
+            out = dot_nn(raised.astype(bf16), v2)
+            outs.append(out * (1.0 / total))
+            sums = jnp.where(lane_q == 2 * pair + half, highest + jnp.log(total), sums)
+        logsum_ref[qrows, :] = sums
+        mixed_ref[qrows, cols] = jnp.where(lane_q < HD, outs[0], outs[1]).astype(bf16)
+
+
+def attend_backward(index, query_const, key_const, q_ref, k_ref, v_ref, mixed_ref, logsum_ref, mixed_grad_ref,
+                    dq_ref, dk_ref, dv_ref, tile):
+    pair, block = index // 2, index % 2
+    cols = pl.ds(pl.multiple_of(pair * LANES, LANES), LANES)
+    rows = pl.ds(pl.multiple_of(block * LONG, LONG), LONG)
+    lane = lane_index(LONG)
+    q2, dm2 = q_ref[rows, cols], mixed_grad_ref[rows, cols]
+    product = dm2.astype(f32) * mixed_ref[rows, cols].astype(f32)
+    sums = logsum_ref[rows, :]
+    qc = query_const[rows, :]
+    zero = jnp.zeros((LONG, LANES), bf16)
+    q_aug, d_aug = [], []
+    for half in range(2):
+        mine = (lane // HD) == half
+        at = lane & (HD - 1)
+        logsum = jnp.sum(jnp.where(lane == 2 * pair + half, sums, 0.0), axis=1, keepdims=True)
+        delta = jnp.sum(jnp.where(mine, product, 0.0), axis=1, keepdims=True)
+        lh, lm, ll = three_parts(-logsum, LONG)
+        dh, dm, dl = three_parts(-delta, LONG)
+        extra = jnp.where(at == 0, lh, jnp.where(at == 1, lm, jnp.where(at == 2, ll, qc)))
+        q_aug.append(jnp.where(mine, q2, extra))
+        extra = jnp.where(at == 0, dh, jnp.where(at == 1, dm, jnp.where(at == 2, dl, zero)))
+        d_aug.append(jnp.where(mine, dm2, extra))
+    dq = [jnp.zeros((LONG, LANES), f32) for _ in range(2)]
+    lane_t = lane_index(tile)
+    one = jnp.ones((tile, LANES), bf16)
+    zero_t = jnp.zeros((tile, LANES), bf16)
+    for t in range(LONG // tile):
+        krows = pl.ds(pl.multiple_of(block * LONG + t * tile, tile), tile)
+        k2, v2, kc = k_ref[krows, cols], v_ref[krows, cols], key_const[krows, :]
+        vc = jnp.where((lane_t & (HD - 1)) < 3, one, zero_t)
+        dk, dv = [], []
+        for half in range(2):
+            mine = (lane_t // HD) == half
+            weights = jnp.exp(dot_nt(jnp.where(mine, k2, kc), q_aug[half]))
+            grads = weights * dot_nt(jnp.where(mine, v2, vc), d_aug[half])
+            low, low_grads = weights.astype(bf16), grads.astype(bf16)
+            dv.append(dot_nn(low, dm2))
+            dk.append(dot_nn(low_grads, q2))
+            dq[half] = dq[half] + dot_tn(low_grads, k2)
+        dk_ref[krows, cols] = jnp.where(lane_t < HD, dk[0], dk[1]).astype(bf16)
+        dv_ref[krows, cols] = jnp.where(lane_t < HD, dv[0], dv[1]).astype(bf16)
+    dq_ref[rows, cols] = (jnp.where(lane < HD, dq[0], dq[1]).astype(bf16).astype(f32) * 0.125).astype(bf16)
+
+
+def gelu_parts(x):
+    z = jnp.abs(x) * 0.7071067811865476
+    t = 1.0 / (1.0 + 0.3275911 * z)
+    bell = jnp.exp(-z * z)
+    tail = t * (0.127414796 + t * (-0.142248368 + t * (0.7107068705 + t * (-0.7265760135 + t * 0.5307027145)))) * bell
+    phi = jnp.where(x >= 0.0, 1.0 - tail, tail)
+    return x * phi, phi + x * (bell * 0.3989422804014327)
+
+
+def norm_parts(x):
+    center = x - jnp.mean(x, axis=-1, keepdims=True)
+    spread = jnp.mean(center * center, axis=-1, keepdims=True)
+    rstd = lax.rsqrt(spread + epsilon)
+    return center * rstd, rstd
+
+
+def norm_back(dy_hat, x_hat, rstd):
+    a = jnp.mean(dy_hat, axis=-1, keepdims=True)
+    b = jnp.mean(dy_hat * x_hat, axis=-1, keepdims=True)
+    return rstd * (dy_hat - a - x_hat * b)
+
+MESH = pl.DeviceIdType.MESH
+Z, X, Y = 4, 2, 2
+CHIPS = Z * Y * X
+JOBS = 6
+PART = FF // JOBS
+BLOCK = D // CHIPS
+FF_BLOCK = FF // CHIPS
+SLICE = FF_BLOCK // JOBS
+ALL = slice(None)
+
+
+def aligned(value, unit):
+    return pl.multiple_of(value, unit)
+
+
+class Place:
+    def __init__(self):
+        group, inner = lax.axis_index("group"), lax.axis_index("inner")
+        self.z, self.y, self.x, self.c = group // Y, group % Y, inner // 2, inner % 2
+        self.index = group * (X * 2) + inner
+        self.chip = group * X + self.x
+        self.twin = (group, self.x * 2 + 1 - self.c)
+        self.over = {
+            "x": ((1 - self.x, (group, (1 - self.x) * 2 + self.c)),),
+            "y": ((1 - self.y, (self.z * Y + 1 - self.y, inner)),),
+            "z": tuple(
+                (z, (z * Y + self.y, inner))
+                for z in (self.z + 1 - 2 * (self.z % 2), (self.z + 2) % Z, Z - 1 - self.z)
+            ),
+        }
+        self.peers = (self.twin,) + tuple(peer for axis in "xyz" for _, peer in self.over[axis])
+
+    def greet(self):
+        barrier = pltpu.get_barrier_semaphore()
+        for peer in self.peers:
+            pl.semaphore_signal(barrier, 1, device_id=peer, device_id_type=MESH)
+
+    def met(self):
+        pl.semaphore_wait(pltpu.get_barrier_semaphore(), len(self.peers))
+
+    def at(self, whole, **given):
+        return tuple(given[a] if a in given else ALL if a in whole else getattr(self, a) for a in "zyx")
+
+
+def remote(source, target, send, recv, peer):
+    return pltpu.make_async_remote_copy(
+        src_ref=source, dst_ref=target, send_sem=send, recv_sem=recv, device_id=peer, device_id_type=MESH
+    )
+
+
+class Cut:
+    def __init__(self, rows, cols, order=None, near=(ALL, ALL)):
+        self.rows, self.cols, self.order, self.near = rows, cols, order, near
+
+
+def row_parts(start, low, high, cols):
+    return (
+        Cut(pl.ds(aligned(start, 16), low), cols, "zxy", (pl.ds(0, low), ALL)),
+        Cut(pl.ds(aligned(start + low, 16), high), cols, "zyx", (pl.ds(low, high), ALL)),
+    )
+
+
+def attend_cuts(core, g):
+    cols = pl.ds(aligned(256 * g + 128 * core, 128), 128)
+    low, high = (16, 32) if g % 2 == 0 else (32, 16)
+    return Cut(pl.ds(0, BLOCK), cols), row_parts(0, low, high, cols)
+
+
+def merge_cuts(core):
+    cols = pl.ds(aligned(384 * core, 128), 384)
+    return Cut(pl.ds(0, BLOCK), cols), row_parts(0, 32, 16, cols)
+
+
+def expand_cuts(core, j):
+    at = PART * j + 256 * core
+    rows = pl.ds(0, BLOCK)
+    return Cut(rows, pl.ds(aligned(at, 128), 256)), tuple(
+        Cut(rows, pl.ds(aligned(at + 128 * n, 128), 128), EXPAND_ORDERS[n], (ALL, pl.ds(128 * n, 128)))
+        for n in range(2)
+    )
+
+
+EXPAND_ORDERS = ("xzy", "yzx")
+
+
+def shrink_cuts(core, j):
+    cols = pl.ds(aligned(384 * core, 128), 384)
+    half = SLICE // 2
+    return Cut(pl.ds(aligned(SLICE * j, SLICE), SLICE), cols), row_parts(SLICE * j, half, half, cols)
+
+
+def blocks(ref, at, cut):
+    deep = (ALL,) if len(ref.shape) == 6 else ()
+    return ref.at[at + deep + (cut.rows, cut.cols)]
+
+
+class Gather:
+    def __init__(self, place, ref, cuts, send, recv, twin_send, twin_recv):
+        self.place, self.ref, (self.whole, self.parts) = place, ref, cuts
+        self.send, self.recv, self.twin_send, self.twin_recv = send, recv, twin_send, twin_recv
+
+    def stage(self, n, part, step):
+        axis = part.order[step]
+        here = blocks(self.ref, self.place.at(part.order[:step]), part)
+        first = sum(len(self.place.over[a]) for a in part.order[:step])
+        return [
+            remote(here, here, self.send.at[n, first + m], self.recv.at[n, first + m], peer)
+            for m, (_, peer) in enumerate(self.place.over[axis])
+        ]
+
+    def to_twin(self):
+        here = blocks(self.ref, self.place.at("zyx"), self.whole)
+        return remote(here, here, self.twin_send, self.twin_recv, self.place.twin)
+
+    def run(self, step):
+        for n, part in enumerate(self.parts):
+            if step > 0:
+                for copy in self.stage(n, part, step - 1):
+                    copy.wait_recv()
+            if step < 3:
+                for copy in self.stage(n, part, step):
+                    copy.start()
+        if step == 3:
+            self.to_twin().start()
+
+    def ready(self):
+        self.to_twin().wait_recv()
+
+    def finish(self):
+        for n, part in enumerate(self.parts):
+            for step in range(3):
+                for copy in self.stage(n, part, step):
+                    copy.wait_send()
+        self.to_twin().wait_send()
+
+
+class Reduce:
+    def __init__(self, place, ref, lands, final, cuts, twin_cuts, sems):
+        self.place, self.ref, (self.whole, self.parts), self.twin_whole = place, ref, cuts, twin_cuts[0]
+        self.lands, self.final = lands, final
+        self.send, self.recv, self.twin_send, self.twin_recv = sems
+        self.deep = (ALL,) if len(ref.shape) == 6 else ()
+
+    def twin(self):
+        source = blocks(self.ref, self.place.at("zyx"), self.twin_whole)
+        return remote(source, self.lands[0], self.twin_send, self.twin_recv, self.place.twin)
+
+    def land(self, part, step, m):
+        ref = self.lands[step]
+        axis, left = part.order[3 - step], part.order[: 3 - step]
+        if step == 1:
+            lead = (ALL, ALL)
+        elif step == 2:
+            lead = (m, ALL) if axis == "z" else (ALL,)
+        else:
+            lead = (m,)
+        if step == 2 and axis != "z":
+            ref = self.lands[4]
+        return ref.at[lead + self.deep + part.near]
+
+    def stage(self, n, part, step):
+        axis, left = part.order[3 - step], part.order[: 3 - step]
+        first = sum(len(self.place.over[a]) for a in part.order[4 - step :])
+        return [
+            remote(
+                blocks(self.ref, self.place.at(left, **{axis: there}), part), self.land(part, step, m),
+                self.send.at[n, first + m], self.recv.at[n, first + m], peer,
+            )
+            for m, (there, peer) in enumerate(self.place.over[axis])
+        ]
+
+    def run(self, step):
+        if step == 0:
+            self.twin().start()
+            return
+        if step == 1:
+            self.twin().wait_recv()
+            mine = blocks(self.ref, self.place.at("zyx"), self.whole)
+            mine[...] = (mine[...].astype(f32) + self.lands[0][...].astype(f32)).astype(bf16)
+        for n, part in enumerate(self.parts):
+            if step > 1:
+                left = part.order[: 4 - step]
+                mine = blocks(self.ref, self.place.at(left), part)
+                value = mine[...].astype(f32)
+                for m, copy in enumerate(self.stage(n, part, step - 1)):
+                    copy.wait_recv()
+                    value += self.land(part, step - 1, m)[...].astype(f32)
+                if step < 4:
+                    mine[...] = value.astype(bf16)
+                else:
+                    self.final[self.deep + (part.rows, part.cols)] = value
+            if step < 4:
+                for copy in self.stage(n, part, step):
+                    copy.start()
+
+    def finish(self):
+        self.twin().wait_send()
+        for n, part in enumerate(self.parts):
+            for step in (1, 2, 3):
+                for copy in self.stage(n, part, step):
+                    copy.wait_send()
+
+T = TOK_DEV
+VEC_ROWS = 16
+PIECES = 8
+ROW_MERGE, ROW_EXPAND, ROW_SHRINK, ROW_GAIN, ROW_SHIFT = 2, 3, 9, 10, 12
+HALF, FF_HALF = BLOCK // 2, FF_BLOCK // 2
+PACK = 3 * D + D + FF
+GATHERS = 4 + 2 * JOBS
+WEIGHTS = (
+    ((Z, Y, X, 3, BLOCK, D), bf16),
+    ((Z, Y, X, BLOCK, D), bf16),
+    ((Z, Y, X, BLOCK, FF), bf16),
+    ((Z, Y, X, FF_BLOCK, D), bf16),
+)
+VMEM_LIMIT = 255 * 2**18
+
+G_START = [(0, 0), (0, 1), (1, 0), (0, 5), (0, 2), (1, 1), (2, 1), (2, 0), (0, 3), (1, 2), (0, 6), (0, 4), (1, 3), (1, 5), (3, 0), (2, 2), (1, 4)]
+G_HEADS = {
+    1: [(1, 6)],
+    2: [(2, 3)],
+    3: [(3, 1)],
+    4: [],
+    5: [(3, 2), (0, 8), (1, 7)],
+    7: [(2, 4)],
+    8: [],
+    9: [(2, 6), (3, 5), (0, 9), (3, 3)],
+    10: [(1, 8)],
+}
+G_READY = {
+    0: [(0, 7)],
+    4: [(2, 5)],
+}
+G_MERGE = [(3, 4), (2, 7)]
+G_FFN = {
+    1: [(3, 6), (2, 8)],
+    4: [(3, 9)],
+}
+G_FFN_MIDDLE = {
+    0: [(1, 9)],
+    2: [(2, 9), (3, 7), (3, 8)],
+}
+R_FFN = {
+}
+R_FFN_MIDDLE = {
+    1: [(1, 0)],
+    2: [(1, 1)],
+    3: [(1, 2)],
+    4: [(2, 0), (2, 1), (1, 3)],
+    5: [(1, 4)],
+}
+R_NORM = {
+    0: [(2, 2)],
+}
+R_MERGE = []
+R_HEADS = {
+    2: [(2, 4), (1, 5)],
+    4: [(2, 3)],
+    5: [(3, 2)],
+    6: [(2, 5)],
+    7: [(3, 1), (2, 6), (3, 0), (1, 7)],
+    8: [(3, 4)],
+    9: [(1, 8)],
+    11: [(3, 6), (4, 0)],
+}
+R_HEADS_END = {
+    3: [(1, 6)],
+    7: [(3, 3)],
+    11: [(2, 8)],
+}
+R_TAIL = [[(3, 5), (2, 7), (1, 9), (4, 2), (3, 8), (4, 6)], [(4, 5)], [(3, 7), (4, 1), (4, 3), (2, 9), (3, 9), (4, 4), (4, 7), (4, 8)], [(4, 9)]]
+
+def chosen(width, offset, start=0):
+    source = lax.broadcasted_iota(jnp.int32, (LANES, D), 0)
+    target = lax.broadcasted_iota(jnp.int32, (LANES, D), 1)
+    mine = (source >= start) & (source < start + width)
+    return jnp.where((target == source + (offset - start)) & mine, 1.0, 0.0).astype(bf16)
+
+
+def vector_maps(place):
+    per_row = D // (2 * HALF)
+    return (
+        chosen(2 * HALF, 2 * HALF * (place.index % per_row)),
+        chosen(HALF, HALF * place.index),
+        [chosen(SLICE, SLICE * place.chip, SLICE * n) for n in range(3)],
+        place.index // per_row,
+    )
+
+
+def place_vectors(place, pieces_ref, out_ref):
+    pieces = pieces_ref[...].astype(bf16)
+    attend_map, single_map, expand_maps, half = vector_maps(place)
+    attend = dot_nn(pieces, attend_map)
+    single = dot_nn(pieces, single_map)
+    expand = jnp.concatenate([dot_nn(pieces, m)[2:3] for m in expand_maps], axis=0)
+    out_ref[...] = jnp.concatenate(
+        [
+            jnp.where(half == 0, attend[0:1], 0.0),
+            jnp.where(half == 1, attend[0:1], 0.0),
+            single[1:2],
+            jnp.where(place.c == 0, expand, 0.0),
+            jnp.where(place.c == 1, expand, 0.0),
+            single[3:8],
+            jnp.zeros((2, D), f32),
+        ],
+        axis=0,
+    ).astype(bf16)
+
+
+def own_vectors(place, sums):
+    attend_map, single_map, expand_maps, half = vector_maps(place)
+    high = sums.astype(bf16)
+    rest = sums - high.astype(f32)
+    middle = rest.astype(bf16)
+    low = (rest - middle.astype(f32)).astype(bf16)
+    parts = jnp.concatenate([high, middle, low], axis=0)
+
+    def pick(chosen_map):
+        found = dot_nt(parts, chosen_map)
+        return found[:VEC_ROWS] + found[VEC_ROWS : 2 * VEC_ROWS] + found[2 * VEC_ROWS :]
+
+    attend, single = pick(attend_map), pick(single_map)
+    expand = 0.0
+    for n, chosen_map in enumerate(expand_maps):
+        found = pick(chosen_map)
+        expand += jnp.where(place.c == 0, found[ROW_EXPAND + n], found[ROW_EXPAND + 3 + n])[None]
+    return jnp.concatenate(
+        [
+            jnp.where(half == 0, attend[0:1], attend[1:2]),
+            single[ROW_MERGE : ROW_MERGE + 1],
+            expand,
+            single[ROW_SHRINK : ROW_SHIFT + 2],
+        ],
+        axis=0,
+    )
+
+
+def lane_groups(read, write, moves):
+    for target, sources in enumerate(moves):
+        parts = []
+        for group, (tile, at) in enumerate(sources):
+            value = read(tile)
+            shift = (group - at) * SLICE % LANES
+            parts.append(pltpu.roll(value, shift, 1) if shift else value)
+        lane = lax.broadcasted_iota(jnp.int32, parts[0].shape, 1) // SLICE
+        write(target, jnp.where(lane < 2, jnp.where(lane == 0, parts[0], parts[1]), jnp.where(lane == 2, parts[2], parts[3])))
+
+
+def ff_moves(inverse):
+    outer, inner = (JOBS, CHIPS) if not inverse else (CHIPS, JOBS)
+    units = [b * outer + a for a in range(outer) for b in range(inner)]
+    return [[(u // 4, u % 4) for u in units[4 * t : 4 * t + 4]] for t in range(FF // LANES)]
+
+
+def compose(place, pack_ref, twin_ref, source_cols):
+    mine = pack_ref[:, source_cols].astype(f32)[:HALF]
+    other = twin_ref[:, source_cols].astype(f32)[:HALF]
+    first = jnp.where(place.c == 0, mine, other)
+    second = jnp.where(place.c == 0, other, mine)
+    return jnp.concatenate([first, second], axis=0).astype(bf16)
+
+
+def layer_kernel(
+    bucket, lengths, keeps, x_any, g_any, attend_ref, merge_ref, expand_ref, shrink_ref, pieces_ref,
+    out_any, ig_any, ga_out, gm_out, ge_out, gs_out, vec_out, active_any, slope_any,
+    wa, wm, we, ws, ga, pack, pack_twin, vec_parts, vec_land, vec,
+    x, g, q, k, v, query_const, key_const, mixed, logsum, xhat, low, xt, lowt, active, slope, first,
+    a0, a1, a3, a4, m0, m1, m3, m4, e0, e1, e2, e3, s0, s1, s3, s4, fa, fm, fe, fs, gain, gain_land,
+    g_send, g_recv, gt_send, gt_recv, r_send, r_recv, rt_send, rt_recv, own_send, own_recv, vec_send, vec_recv,
+    sum_send, sum_recv, last_send, last_recv, local, flow,
+):
+    place = Place()
+    c = place.c
+    place.greet()
+    x_copy = pltpu.make_async_copy(x_any, x, local.at[0])
+    g_copy = pltpu.make_async_copy(g_any, g, local.at[1])
+    x_copy.start()
+    g_copy.start()
+
+    pack[0:HALF, 0 : 3 * D] = attend_ref[...]
+    pack[0:HALF, 3 * D : 4 * D] = merge_ref[...]
+
+    def put_expand(tile, value):
+        pack[0:HALF, 4 * D + LANES * tile : 4 * D + LANES * (tile + 1)] = value.astype(bf16)
+
+    lane_groups(
+        lambda tile: expand_ref[:, LANES * tile : LANES * (tile + 1)].astype(f32), put_expand, ff_moves(False)
+    )
+    place_vectors(place, pieces_ref, vec_parts.at[0])
+    token_tables(
+        bucket[0], [lengths[0, b] for b in range(SLOTS)], [keeps[0, b] for b in range(SLOTS)],
+        query_const, key_const, logsum,
+    )
+    x_copy.wait()
+    xt[...] = x[...].T
+    place.met()
+
+    own_pack = remote(pack, pack_twin, own_send.at[0], own_recv.at[0], place.twin)
+    own_pack.start()
+    their_cols = pl.ds(aligned(384 * (1 - c), 128), 384)
+    my_cols = pl.ds(aligned(384 * c, 128), 384)
+    my_rows = pl.ds(aligned(FF_HALF * c, FF_HALF), FF_HALF)
+    own_shrink = remote(
+        shrink_ref.at[:, their_cols], ws.at[place.z, place.y, place.x, my_rows, their_cols],
+        own_send.at[1], own_recv.at[1], place.twin,
+    )
+
+    def vec_copy(source, land, sends, recvs, step, m, peer):
+        return remote(source.at[step], land.at[step + m], sends.at[step + m], recvs.at[step + m], peer)
+
+    def vec_chain(source, land, sends, recvs):
+        steps = [(place.twin,)] + [tuple(peer for _, peer in place.over[a]) for a in "xyz"]
+        return [[vec_copy(source, land, sends, recvs, s, m, p) for m, p in enumerate(peers)] for s, peers in enumerate(steps)]
+
+    vec_steps = vec_chain(vec_parts, vec_land, vec_send, vec_recv)
+    sum_steps = vec_chain(gain, gain_land, sum_send, sum_recv)
+
+    def add_next(steps, source, land, step):
+        steps[step][0].wait_recv()
+        source[step + 1] = (source[step].astype(f32) + land[step].astype(f32)).astype(source.dtype)
+        for copy in steps[step + 1]:
+            copy.start()
+
+    def add_last(steps, source, land):
+        total = source[3].astype(f32)
+        for m, copy in enumerate(steps[3]):
+            copy.wait_recv()
+            total += land[3 + m].astype(f32)
+        return total
+
+    vec_steps[0][0].start()
+    own_shrink.start()
+
+    def gathers(t):
+        def one(ref, cuts, at):
+            return Gather(place, ref, cuts, g_send.at[at], g_recv.at[at], gt_send.at[at], gt_recv.at[at])
+
+        if t < 3:
+            return [one(wa, attend_cuts(c, t), t)]
+        if t == 3:
+            return [one(wm, merge_cuts(c), 3)]
+        j = t - 4
+        return [one(we, expand_cuts(c, j), 4 + 2 * j), one(ws, shrink_cuts(c, j), 5 + 2 * j)]
+
+    def gather_events(names):
+        for step, t in names:
+            for one in gathers(t):
+                one.run(step)
+
+    def when(index, table, events):
+        for value, names in table.items():
+
+            @pl.when(index == value)
+            def _():
+                events(names)
+
+    own_pack.wait_recv()
+    for group in range(3):
+        for n in range(3):
+            cols = aligned(256 * group + 128 * c, 128)
+            wa[place.z, place.y, place.x, n, :, pl.ds(cols, 128)] = compose(
+                place, pack, pack_twin, pl.ds(aligned(D * n + cols, 128), 128)
+            )
+    wm[place.z, place.y, place.x, :, my_cols] = compose(
+        place, pack, pack_twin, pl.ds(aligned(3 * D + 384 * c, 128), 384)
+    )
+    for j in range(JOBS):
+        cols = aligned(PART * j + 256 * c, 128)
+        we[place.z, place.y, place.x, :, pl.ds(cols, 256)] = compose(
+            place, pack, pack_twin, pl.ds(aligned(4 * D + cols, 128), 256)
+        )
+    ws[place.z, place.y, place.x, my_rows, my_cols] = shrink_ref[:, my_cols]
+    own_shrink.wait_recv()
+    gather_events(G_START[:2])
+    add_next(vec_steps, vec_parts, vec_land, 0)
+    gather_events(G_START[2:4])
+    add_next(vec_steps, vec_parts, vec_land, 1)
+    gather_events(G_START[4:8])
+    add_next(vec_steps, vec_parts, vec_land, 2)
+    gather_events(G_START[8:])
+    vec[...] = add_last(vec_steps, vec_parts, vec_land)
+
+    def heads(i, carry):
+        when(i, G_HEADS, gather_events)
+        for group in range(3):
+
+            @pl.when(i == 4 * group)
+            def _():
+                for one in gathers(group):
+                    one.ready()
+
+        @pl.when(i % 4 == 0)
+        def _():
+            cols = pl.ds(aligned(256 * (i // 4), 256), 256)
+            tokens = x[...]
+            part = dot_nn(tokens, wa[:, :, :, 0, :, cols].reshape(D, 256))
+            q[:, cols] = ((part + vec[0:1, cols]) * 0.125).astype(bf16)
+            k[:, cols] = dot_nn(tokens, wa[:, :, :, 1, :, cols].reshape(D, 256)).astype(bf16)
+            part = dot_nn(tokens, wa[:, :, :, 2, :, cols].reshape(D, 256))
+            v[:, cols] = (part + vec[1:2, cols]).astype(bf16)
+
+        when(i, G_READY, gather_events)
+        attend_forward(i, query_const, key_const, q, k, v, mixed, logsum, LONG)
+        return carry
+
+    lax.fori_loop(0, 12, heads, 0)
+    gather_events(G_MERGE)
+    for one in gathers(3):
+        one.ready()
+    tile = 512
+
+    def merge_norm(i, carry):
+        rows = pl.ds(aligned(i * tile, tile), tile)
+        branch = dot_nn(mixed[rows, :], wm[...].reshape(D, D)) + vec[ROW_MERGE : ROW_MERGE + 1, :]
+        x_hat, deviation = norm_parts(x[rows, :].astype(f32) + branch)
+        xhat[rows, :] = x_hat.astype(bf16)
+        logsum[rows, :] = jnp.where(lane_index(tile) == RSTD_LANE, deviation, logsum[rows, :])
+        normed = x_hat * vec[ROW_GAIN : ROW_GAIN + 1, :] + vec[ROW_SHIFT : ROW_SHIFT + 1, :]
+        low[rows, :] = normed.astype(bf16)
+        first[rows, :] = normed + vec[ROW_SHRINK : ROW_SHRINK + 1, :]
+        return carry
+
+    lax.fori_loop(0, T // tile, merge_norm, 0)
+    lowt[...] = low[...].T
+
+    def out_copies(j):
+        return (
+            pltpu.make_async_copy(active.at[j % 2], active_any.at[j], flow.at[0, j % 2]),
+            pltpu.make_async_copy(slope.at[j % 2], slope_any.at[j], flow.at[1, j % 2]),
+        )
+
+    def back_copies(j):
+        return (
+            pltpu.make_async_copy(active_any.at[j], active.at[j % 2], flow.at[0, j % 2]),
+            pltpu.make_async_copy(slope_any.at[j], slope.at[j % 2], flow.at[1, j % 2]),
+        )
+
+    def expand_part(j, carry):
+        when(j, G_FFN, gather_events)
+
+        @pl.when(j >= 2)
+        def _():
+            for copy in out_copies(j - 2):
+                copy.wait()
+
+        for t in range(JOBS):
+
+            @pl.when(j == t)
+            def _():
+                for one in gathers(4 + t):
+                    one.ready()
+
+        a_ref, s_ref = active.at[j % 2], slope.at[j % 2]
+        for h in range(2):
+            here = slice(256 * h, 256 * h + 256)
+            cols = pl.ds(aligned(PART * j + 256 * h, 256), 256)
+            bias = vec[pl.ds(ROW_EXPAND + j, 1), here]
+            expanded = dot_nn(low[...], we[:, :, :, :, cols].reshape(D, 256)) + bias
+            a, s = gelu_parts(expanded)
+            a_ref[:, here] = a.astype(bf16)
+            s_ref[:, here] = s.astype(bf16)
+        when(j, G_FFN_MIDDLE, gather_events)
+        rows = pl.ds(aligned(SLICE * j, SLICE), SLICE)
+        first[...] += dot_nn(a_ref[...], ws[:, :, :, rows, :].reshape(PART, D))
+
+        @pl.when(j < JOBS - 2)
+        def _():
+            for copy in out_copies(j):
+                copy.start()
+
+        return carry
+
+    lax.fori_loop(0, JOBS, expand_part, 0)
+    g_copy.wait()
+    gain[0] = jnp.zeros((VEC_ROWS, D), f32)
+
+    def end_of_forward(i, carry):
+        rows = pl.ds(aligned(i * tile, tile), tile)
+        x_hat, deviation = norm_parts(first[rows, :])
+        weight = vec[ROW_GAIN + 1 : ROW_GAIN + 2, :]
+        result = x_hat * weight + vec[ROW_SHIFT + 1 : ROW_SHIFT + 2, :]
+        keep = column_of(logsum[rows, :], KEEP_LANE) > 0.0
+        dy = jnp.where(keep, g[rows, :].astype(f32), 0.0)
+        g[rows, :] = jnp.where(keep, result, x[rows, :].astype(f32)).astype(bf16)
+        grad = norm_back(dy * weight, x_hat, deviation)
+        first[rows, :] = grad
+        branch = grad.astype(bf16)
+        low[rows, :] = branch
+        gain[0, ROW_GAIN + 1 : ROW_GAIN + 2, :] += jnp.sum(dy * x_hat, axis=0, keepdims=True)
+        gain[0, ROW_SHIFT + 1 : ROW_SHIFT + 2, :] += jnp.sum(dy, axis=0, keepdims=True)
+        gain[0, ROW_SHRINK : ROW_SHRINK + 1, :] += jnp.sum(branch.astype(f32), axis=0, keepdims=True)
+        return carry
+
+    lax.fori_loop(0, T // tile, end_of_forward, 0)
+    out_copy = pltpu.make_async_copy(g, out_any, local.at[2])
+    out_copy.start()
+
+    def reductions(t):
+        def one(ref, lands, final, cuts, at, *args):
+            sems = (r_send.at[at], r_recv.at[at], rt_send.at[at], rt_recv.at[at])
+            return Reduce(place, ref, lands, final, cuts(c, *args), cuts(1 - c, *args), sems)
+
+        if t < JOBS:
+            j = JOBS - 1 - t
+            return [
+                one(we, [e0.at[t % 2], e1.at[t], e2.at[t], e3.at[t], None], fe, expand_cuts, 2 * t, j),
+                one(ws, [s0.at[t % 2], s1.at[t], None, s3.at[t], s4.at[t]], fs, shrink_cuts, 2 * t + 1, j),
+            ]
+        if t == JOBS:
+            return [one(wm, [m0, m1, None, m3, m4], fm, merge_cuts, 2 * JOBS)]
+        n = t - JOBS - 1
+        return [one(ga, [a0.at[n % 2], a1.at[n], None, a3.at[n], a4.at[n]], fa, attend_cuts, 2 * JOBS + 1 + n, n)]
+
+    def reduce_events(names):
+        for step, t in names:
+            for one in reductions(t):
+                one.run(step)
+
+    def expand_back(b, carry):
+        j = JOBS - 1 - b
+
+        @pl.when(b >= 2)
+        def _():
+            for copy in back_copies(j):
+                copy.wait()
+
+        when(b, R_FFN, reduce_events)
+        a_ref, s_ref = active.at[j % 2], slope.at[j % 2]
+        rows = pl.ds(aligned(SLICE * j, SLICE), SLICE)
+        cols = pl.ds(aligned(PART * j, PART), PART)
+        s_in = low[...]
+        for h in range(2):
+            here = slice(256 * h, 256 * h + 256)
+            e_in = dot_nt(s_in, ws[2 * h : 2 * h + 2, :, :, rows, :].reshape(256, D)) * s_ref[:, here].astype(f32)
+            e_in = e_in.astype(bf16)
+            s_ref[:, here] = e_in
+            gain[0, pl.ds(ROW_EXPAND + j, 1), here] = jnp.sum(e_in.astype(f32), axis=0, keepdims=True)
+        when(b, R_FFN_MIDDLE, reduce_events)
+        for h in range(2):
+            grad = dot_tn(a_ref[:, 256 * h : 256 * h + 256], s_in).astype(bf16)
+            ws[2 * h : 2 * h + 2, :, :, rows, :] = grad.reshape(2, Y, X, SLICE, D)
+        first[...] += dot_nt(s_ref[...], we[:, :, :, :, cols].reshape(D, PART))
+        for h in range(2):
+            here = pl.ds(aligned(PART * j + 256 * h, 256), 256)
+            grad = dot_nn(lowt[...], s_ref[:, 256 * h : 256 * h + 256]).astype(bf16)
+            we[:, :, :, :, here] = grad.reshape(Z, Y, X, BLOCK, 256)
+        when(b, {t: [(0, t)] for t in range(JOBS)}, reduce_events)
+
+        @pl.when(b < JOBS - 2)
+        def _():
+            for copy in back_copies(j - 2):
+                copy.start()
+
+        return carry
+
+    for t in range(4 + JOBS):
+        for one in gathers(t):
+            one.finish()
+    lax.fori_loop(0, JOBS, expand_back, 0)
+
+    def middle(i, carry):
+        when(i, R_NORM, reduce_events)
+        rows = pl.ds(aligned(i * tile, tile), tile)
+        dy, x_hat = first[rows, :], xhat[rows, :].astype(f32)
+        deviation = column_of(logsum[rows, :], RSTD_LANE)
+        grad = norm_back(dy * vec[ROW_GAIN : ROW_GAIN + 1, :], x_hat, deviation)
+        first[rows, :] = grad
+        branch = grad.astype(bf16)
+        low[rows, :] = branch
+        gain[0, ROW_GAIN : ROW_GAIN + 1, :] += jnp.sum(dy * x_hat, axis=0, keepdims=True)
+        gain[0, ROW_SHIFT : ROW_SHIFT + 1, :] += jnp.sum(dy, axis=0, keepdims=True)
+        gain[0, ROW_MERGE : ROW_MERGE + 1, :] += jnp.sum(branch.astype(f32), axis=0, keepdims=True)
+        x[rows, :] = dot_nt(branch, wm[...].reshape(D, D)).astype(bf16)
+        return carry
+
+    lax.fori_loop(0, T // tile, middle, 0)
+    out_copy.wait()
+    g_again = pltpu.make_async_copy(g_any, g, local.at[1])
+    g_again.start()
+    reduce_events(R_MERGE)
+    wm[...] = dot_tn(mixed[...], low[...]).astype(bf16).reshape(Z, Y, X, BLOCK, D)
+    reduce_events([(0, JOBS)])
+
+    def heads_back(i, carry):
+        when(i, R_HEADS, reduce_events)
+        attend_backward(i, query_const, key_const, q, k, v, mixed, logsum, x, q, k, v, LONG)
+
+        when(i, R_HEADS_END, reduce_events)
+
+        @pl.when(i % 4 == 3)
+        def _():
+            cols = pl.ds(aligned(256 * (i // 4), 256), 256)
+            for n, grads in enumerate((q, k, v)):
+                grad = dot_nn(xt[...], grads[:, cols]).astype(bf16)
+                ga[:, :, :, n, :, cols] = grad.reshape(Z, Y, X, BLOCK, 256)
+                if n != 1:
+                    gain[0, n // 2 : n // 2 + 1, cols] = jnp.sum(grads[:, cols].astype(f32), axis=0, keepdims=True)
+
+        when(i, {4 * n + 3: [(0, JOBS + 1 + n)] for n in range(3)}, reduce_events)
+        return carry
+
+    lax.fori_loop(0, 12, heads_back, 0)
+    sum_steps[0][0].start()
+
+    def last_copy(ref, n, cols, height):
+        rows = pl.ds(aligned(height * (1 - c), 8), height)
+        here = ref.at[:, rows, cols] if len(ref.shape) == 3 else ref.at[rows, cols]
+        return remote(here, here, last_send.at[n], last_recv.at[n], place.twin)
+
+    early_last = [last_copy(fm, 0, my_cols, HALF), last_copy(fs, 1, my_cols, FF_HALF)]
+    early_last += [last_copy(fe, 2 + j, expand_cuts(c, j)[0].cols, HALF) for j in range(JOBS)]
+    attend_last = [last_copy(fa, 2 + JOBS + n, attend_cuts(c, n)[0].cols, HALF) for n in range(3)]
+
+    reduce_events(R_TAIL[0])
+    g_again.wait()
+
+    def inputs_part(i, carry):
+        @pl.when(i == 1)
+        def _():
+            reduce_events(R_TAIL[1])
+            add_next(sum_steps, gain, gain_land, 0)
+
+        rows = pl.ds(aligned(i * tile, tile), tile)
+        keep = column_of(logsum[rows, :], KEEP_LANE) > 0.0
+        total = first[rows, :] + jnp.where(keep, 0.0, g[rows, :].astype(f32))
+        for n, grads in enumerate((q, k, v)):
+            total += dot_nt(grads[rows, :], wa[:, :, :, n, :, :].reshape(D, D))
+        first[rows, :] = total
+        return carry
+
+    lax.fori_loop(0, T // tile, inputs_part, 0)
+    out_ig = pltpu.make_async_copy(first, ig_any, local.at[3])
+    out_ig.start()
+    add_next(sum_steps, gain, gain_land, 1)
+    reduce_events(R_TAIL[2])
+    for copy in early_last + attend_last[:2]:
+        copy.start()
+    add_next(sum_steps, gain, gain_land, 2)
+    mine, ff_mine = pl.ds(aligned(HALF * c, 8), HALF), pl.ds(aligned(FF_HALF * c, 8), FF_HALF)
+    for copy in early_last:
+        copy.wait_recv()
+    gm_out[...] = fm[mine, :]
+    gs_out[...] = fs[ff_mine, :]
+
+    def put_grad(tile, value):
+        ge_out[:, LANES * tile : LANES * (tile + 1)] = value
+
+    lane_groups(lambda tile: fe[mine, LANES * tile : LANES * (tile + 1)], put_grad, ff_moves(True))
+    own_pack.wait_send()
+    own_shrink.wait_send()
+    for copy in early_last + sum(vec_steps + sum_steps[:3], []):
+        copy.wait_send()
+    for t in range(JOBS + 3):
+        for one in reductions(t):
+            one.finish()
+    reduce_events(R_TAIL[3])
+    attend_last[2].start()
+    vec_out[...] = own_vectors(place, add_last(sum_steps, gain, gain_land))
+    for copy in sum_steps[3]:
+        copy.wait_send()
+    for one in reductions(JOBS + 3):
+        one.finish()
+    for copy in attend_last:
+        copy.wait_recv()
+        copy.wait_send()
+    for n in range(3):
+        ga_out[:, D * n : D * n + D] = fa[n, mine, :]
+    out_ig.wait()
+
+
+ANY = pl.BlockSpec(memory_space=pl.ANY)
+VM = pl.BlockSpec(memory_space=pltpu.VMEM)
+SM = pl.BlockSpec(memory_space=pltpu.SMEM)
+
+
+def layer_call(buckets, lengths, keeps, inputs, upstream, attend, merge, expand, shrink, pieces):
+    dma = pltpu.SemaphoreType.DMA
+
+    def landing(rows, cols, jobs=None, deep=(), slots=None, middle=False):
+        lead = (jobs,) if jobs else ()
+        dims = [((slots,) if slots else lead) + (Z, Y, X), lead + (Z, 2)]
+        dims += [lead + (3, 2), lead + (1,)] if middle else [lead + (3,), lead + (Z,)]
+        return [pltpu.VMEM(d + deep + (rows, cols), bf16) for d in dims]
+
+    tokens = [pltpu.VMEM((T, D), bf16) for _ in range(5)]
+    scratch = (
+        [pltpu.VMEM(*s) for s in WEIGHTS]
+        + [
+            pltpu.VMEM(*WEIGHTS[0]),
+            pltpu.VMEM((32, PACK), bf16),
+            pltpu.VMEM((32, PACK), bf16),
+            pltpu.VMEM((4, VEC_ROWS, D), bf16),
+            pltpu.VMEM((6, VEC_ROWS, D), bf16),
+            pltpu.VMEM((VEC_ROWS, D), f32),
+        ]
+        + tokens
+        + [
+            pltpu.VMEM((T, LANES), bf16),
+            pltpu.VMEM((T, LANES), bf16),
+            pltpu.VMEM((T, D), bf16),
+            pltpu.VMEM((T, LANES), f32),
+            pltpu.VMEM((T, D), bf16),
+            pltpu.VMEM((T, D), bf16),
+            pltpu.VMEM((D, T), bf16),
+            pltpu.VMEM((D, T), bf16),
+            pltpu.VMEM((2, T, PART), bf16),
+            pltpu.VMEM((2, T, PART), bf16),
+            pltpu.VMEM((T, D), f32),
+        ]
+        + landing(BLOCK, 128, 3, (3,), slots=2)
+        + landing(BLOCK, 384)
+        + landing(BLOCK, 256, JOBS, slots=2, middle=True)
+        + landing(SLICE, 384, JOBS, slots=2)
+        + [
+            pltpu.VMEM((3, BLOCK, D), f32),
+            pltpu.VMEM((BLOCK, D), f32),
+            pltpu.VMEM((BLOCK, FF), f32),
+            pltpu.VMEM((FF_BLOCK, D), f32),
+            pltpu.VMEM((4, VEC_ROWS, D), f32),
+            pltpu.VMEM((6, VEC_ROWS, D), f32),
+        ]
+        + 2 * [dma((GATHERS, 2, 5)), dma((GATHERS, 2, 5)), dma((GATHERS,)), dma((GATHERS,))]
+        + 2 * [dma((2,))]
+        + 4 * [dma((6,))]
+        + 2 * [dma((5 + JOBS,))]
+        + [dma((4,)), dma((2, 2))]
+    )
+    return pl.pallas_call(
+        layer_kernel,
+        out_shape=tuple(
+            jax.ShapeDtypeStruct(*s)
+            for s in (
+                ((T, D), bf16), ((T, D), f32), ((HALF, 3 * D), f32), ((HALF, D), f32), ((HALF, FF), f32),
+                ((FF_HALF, D), f32), ((PIECES, LANES), f32), ((JOBS, T, PART), bf16), ((JOBS, T, PART), bf16),
+            )
+        ),
+        in_specs=[SM, SM, SM, ANY, ANY, VM, VM, VM, VM, VM],
+        out_specs=[ANY, ANY] + [VM] * 5 + [ANY, ANY],
+        scratch_shapes=scratch,
+        compiler_params=pltpu.CompilerParams(collective_id=0, has_side_effects=True, vmem_limit_bytes=VMEM_LIMIT),
+        cost_estimate=pl.CostEstimate(flops=60_000_000_000, bytes_accessed=60_000_000, transcendentals=20_000_000),
+    )(buckets, lengths, keeps, inputs, upstream, attend, merge, expand, shrink, pieces)
+
+
+def pack_pieces(attend_bias, merge_bias, expand_bias, shrink_bias, gain, shift):
+    total = 0.0
+    vectors = (attend_bias[None], merge_bias[None], expand_bias[None], shrink_bias[None], gain, shift)
+    row = 0
+    for piece in vectors:
+        count, width = piece.shape
+        total += jnp.pad(piece.astype(f32), ((row, PIECES - row - count), (0, LANES - width)))
+        row += count
+    return total
+
+
+def finish_kernel(*refs):
+    count = len(RESULTS)
+    sources, own, wide, vectors = refs[:count], refs[count], refs[count + 1 : 2 * count + 1], refs[2 * count + 1 : -count - 2]
+    held, arrive, leave = refs[-count - 2 : -2], refs[-2], refs[-1]
+    steps = [
+        (pltpu.make_async_copy(s, h, arrive.at[n]), pltpu.make_async_copy(h, w, leave.at[n]))
+        for n, (s, h, w) in enumerate(zip(sources, held, wide))
+    ]
+    for into, _ in steps:
+        into.start()
+    row = 0
+    for ref in vectors:
+        if len(ref.shape) == 1:
+            ref[...] = own[row, : ref.shape[0]]
+            row += 1
+        else:
+            ref[...] = own[row : row + ref.shape[0], : ref.shape[1]]
+            row += ref.shape[0]
+    for into, out in steps:
+        into.wait()
+        out.start()
+    for _, out in steps:
+        out.wait()
+
+
+RESULTS = (
+    ((T, D), f32), ((T, D), bf16), ((HALF, 3 * D), f32), ((HALF, D), f32), ((HALF, FF), f32), ((FF_HALF, D), f32),
+)
+
+
+def finish_call(wide, own, vectors):
+    dma = pltpu.SemaphoreType.DMA
+    return pl.pallas_call(
+        finish_kernel,
+        out_shape=tuple(jax.ShapeDtypeStruct(*s) for s in RESULTS)
+        + tuple(jax.ShapeDtypeStruct(v.shape, f32) for v in vectors),
+        in_specs=[ANY] * len(RESULTS) + [VM],
+        out_specs=[ANY] * len(RESULTS) + [VM] * len(vectors),
+        scratch_shapes=[pltpu.VMEM(*s) for s in RESULTS] + 2 * [dma((len(RESULTS),))],
+        compiler_params=pltpu.CompilerParams(vmem_limit_bytes=VMEM_LIMIT),
+    )(*wide, own)
 
 def layer_norm(hidden, gains, shifts):
     center = hidden - jnp.mean(hidden, axis=-1, keepdims=True)
@@ -241,7 +1294,7 @@
     return (grads, input_grad)
 
 
-def on_device(
+def general_device(
     inputs,
     upstream,
     buckets,
@@ -314,8 +1367,25 @@
         shares[9],
     )
 
+def slice_device(
+    inputs, upstream, buckets, lengths, layer_keep, attend_weight, attend_bias, merge_weight, merge_bias,
+    expand_weight, expand_bias, shrink_weight, shrink_bias, norm_gain, norm_shift,
+):
+    pieces = pack_pieces(attend_bias, merge_bias, expand_bias, shrink_bias, norm_gain, norm_shift)
+    outputs, input_grad, attend, merge, expand, shrink, own = layer_call(
+        buckets, lengths, layer_keep, inputs, upstream, attend_weight, merge_weight, expand_weight, shrink_weight, pieces
+    )[:7]
+    input_grad, outputs, attend, merge, expand, shrink, attend_b, merge_b, expand_b, shrink_b, gain, shift = finish_call(
+        (input_grad, outputs, attend, merge, expand, shrink),
+        own,
+        (attend_bias, merge_bias, expand_bias, shrink_bias, norm_gain, norm_shift),
+    )
+    return (
+        outputs, input_grad, attend, attend_b, merge, merge_b, expand, expand_b, shrink, shrink_b, gain, shift,
+    )
 
 def solution(mesh):
+    on_slice = mesh.shape["group"] == Z * Y and mesh.shape["inner"] == 2 * X
     placed = (
         P(("group", "inner"), None),
         P(("group", "inner"), None),
@@ -334,7 +1404,7 @@
         P(None, ("group", "inner")),
     )
     return jax.shard_map(
-        on_device,
+        slice_device if on_slice else general_device,
         mesh=mesh,
         in_specs=placed,
         out_specs=(

time: 848 us -> 196 us (0.23)
  waiting for transfers between devices: 372 us -> 0 us
  Pallas kernels: 0 us -> 192 us
  matrix products: 175 us -> 0 us
  blocking collectives: 159 us -> 0 us
  local copies, waits for them, and re-layouts: 73.7 us -> 0 us
  other arithmetic: 42.4 us -> 1.34 us
  between operations: 15.8 us -> 1.5 us
    reduce_scatter x3 -> x0, waiting for transfers between devices: 284 us -> none  [the longest x1 142 us: on_device(): lax.psum_scatter(grads[6], ('group', 'inner'), scatter_dimension=0, tiled...]
    pallas_call x0 -> x2, Pallas kernels: none -> 192 us  [the longest x1 187 us: layer_call(): pl.pallas_call(layer_kernel, out_shape=tuple((jax.ShapeDtypeStruct(*s) fo...]
    dot_general x26 -> x0, matrix products: 175 us -> none  [the longest x4 57.6 us: matmul(): return jnp.dot(left, right, preferred_element_type=jnp.float32)]
    unnamed x2 -> x0, blocking collectives: 82.8 us -> none
    all_gather x2 -> x0, blocking collectives: 76.4 us -> none  [the longest x1 40 us: on_device(): lax.all_gather(norm_gain, ('group', 'inner'), axis=1, tiled=True)]
    unnamed x9 -> x0, waiting for transfers between devices: 65.2 us -> none
    unnamed x129 -> x0, local copies, waits for them, and re-layouts: 35.4 us -> none
    all_gather x4 -> x0, waiting for transfers between devices: 23 us -> none  [the longest x1 22.9 us: on_device(): lax.all_gather(shrink_weight, ('group', 'inner'), axis=0, tiled=True)]
  transfers between devices with their start and end apart: 8 -> 0, of which waited for: 4 -> 0; matrix products, arithmetic and copies ran while one was open for 26% -> 0% of each run, Pallas kernels for 0% -> 0%
where the time goes in v2:
time: 196 us; the launch traced here: 195 us
  Pallas kernels  192 us (98%)
    pallas_call x1, Pallas kernels, layer_call(): pl.pallas_call(layer_kernel, out_shape=tuple((jax.ShapeDtypeStruct(*s) fo...  187 us
    pallas_call x1, Pallas kernels, finish_call(): pl.pallas_call(finish_kernel, out_shape=tuple((jax.ShapeDtypeStruct(*s) f...  5.7 us

profile of v2, /device:TPU:0, one launch (start us, length us, event | category | flops | bytes accessed | tf_op | source)
XLA Modules:
  0.0 195.3 jit_solution(13570615969055619161)
XLA Ops:
  1.3 1.3 convert_add_fusion.pieces_ref
  2.6 186.8 %shard_map.238 = (bf16[1024,768]{1,0:T(8,128)(2,1)}, f32[1024,768]{1,0:T(8,128)}, f32[24,2304]{1,0:T(8,128)}, f32[24,768]{1,0:T(8,128)}, f32[24,3072]{1,0:T(8,12...) custom-call(s32[1]{0:T(128)S(6)} %copy.27.bucket, ...), custom_call_target="tpu_custom_call" | custom-call | flops 60000002048 | bytes 60000000 | tf_op jit(solution)/shard_map/pallas_call | solution.py:1001
  189.4 5.7 %shard_map.239 = (f32[1024,768]{1,0:T(8,128)}, bf16[1024,768]{1,0:T(8,128)(2,1)}, f32[24,2304]{1,0:T(8,128)}, f32[24,768]{1,0:T(8,128)}, f32[24,3072]{1,0:T(8,12...) custom-call(f32[1024,768]{1,0:T(8,128)} %get-tuple-element.31.refs_0, ...), custom_call_target="tpu_custom_call" | custom-call | tf_op jit(solution)/shard_map/pallas_call | solution.py:1061

commit v3 on v2

--- a/solution.py
+++ b/solution.py
@@ -151,9 +151,11 @@
 
 
 def gelu_parts(x):
-    z = jnp.abs(x) * 0.7071067811865476
-    t = 1.0 / (1.0 + 0.3275911 * z)
-    bell = jnp.exp(-z * z)
+    magnitude = jnp.abs(x)
+    base = 1.0 + (0.3275911 * 0.7071067811865476) * magnitude
+    t = pl.reciprocal(base, approx=True)
+    t = t * (2.0 - base * t)
+    bell = jnp.exp2(x * x * -0.7213475204444817)
     tail = t * (0.127414796 + t * (-0.142248368 + t * (0.7107068705 + t * (-0.7265760135 + t * 0.5307027145)))) * bell
     phi = jnp.where(x >= 0.0, 1.0 - tail, tail)
     return x * phi, phi + x * (bell * 0.3989422804014327)
@@ -247,13 +249,10 @@
 def expand_cuts(core, j):
     at = PART * j + 256 * core
     rows = pl.ds(0, BLOCK)
+    orders = ("xzy", "zyx") if j % 2 == 0 else ("zxy", "yzx")
     return Cut(rows, pl.ds(aligned(at, 128), 256)), tuple(
-        Cut(rows, pl.ds(aligned(at + 128 * n, 128), 128), EXPAND_ORDERS[n], (ALL, pl.ds(128 * n, 128)))
-        for n in range(2)
-    )
-
-
-EXPAND_ORDERS = ("xzy", "yzx")
+        Cut(rows, pl.ds(aligned(at + 128 * n, 128), 128), orders[n]) for n in range(2)
+    )
 
 
 def shrink_cuts(core, j):
@@ -308,27 +307,20 @@
 
 
 class Reduce:
-    def __init__(self, place, ref, lands, final, cuts, twin_cuts, sems):
+    def __init__(self, place, ref, land0, lands, final, cuts, twin_cuts, sems):
         self.place, self.ref, (self.whole, self.parts), self.twin_whole = place, ref, cuts, twin_cuts[0]
-        self.lands, self.final = lands, final
+        self.land0, self.lands, self.final = land0, lands, final
         self.send, self.recv, self.twin_send, self.twin_recv = sems
         self.deep = (ALL,) if len(ref.shape) == 6 else ()
 
     def twin(self):
         source = blocks(self.ref, self.place.at("zyx"), self.twin_whole)
-        return remote(source, self.lands[0], self.twin_send, self.twin_recv, self.place.twin)
+        return remote(source, self.land0, self.twin_send, self.twin_recv, self.place.twin)
 
     def land(self, part, step, m):
-        ref = self.lands[step]
-        axis, left = part.order[3 - step], part.order[: 3 - step]
-        if step == 1:
-            lead = (ALL, ALL)
-        elif step == 2:
-            lead = (m, ALL) if axis == "z" else (ALL,)
-        else:
-            lead = (m,)
-        if step == 2 and axis != "z":
-            ref = self.lands[4]
+        axis = part.order[3 - step]
+        ref = self.lands[part.order[1] == "z"][step - 1]
+        lead = ((ALL, ALL), (m, ALL) if axis == "z" else (ALL,), (m,))[step - 1]
         return ref.at[lead + self.deep + part.near]
 
     def stage(self, n, part, step):
@@ -349,7 +341,7 @@
         if step == 1:
             self.twin().wait_recv()
             mine = blocks(self.ref, self.place.at("zyx"), self.whole)
-            mine[...] = (mine[...].astype(f32) + self.lands[0][...].astype(f32)).astype(bf16)
+            mine[...] = (mine[...].astype(f32) + self.land0[...].astype(f32)).astype(bf16)
         for n, part in enumerate(self.parts):
             if step > 1:
                 left = part.order[: 4 - step]
@@ -375,6 +367,7 @@
 
 T = TOK_DEV
 VEC_ROWS = 16
+VECTORS = 99
 PIECES = 8
 ROW_MERGE, ROW_EXPAND, ROW_SHRINK, ROW_GAIN, ROW_SHIFT = 2, 3, 9, 10, 12
 HALF, FF_HALF = BLOCK // 2, FF_BLOCK // 2
@@ -388,30 +381,31 @@
 )
 VMEM_LIMIT = 255 * 2**18
 
-G_START = [(0, 0), (0, 1), (1, 0), (0, 5), (0, 2), (1, 1), (2, 1), (2, 0), (0, 3), (1, 2), (0, 6), (0, 4), (1, 3), (1, 5), (3, 0), (2, 2), (1, 4)]
+G_START = [(0, 0), (0, 1), (0, 2), (1, 99), (1, 0), (1, 1), (2, 0), (0, 5), (0, 3), (1, 2), (2, 99), (2, 1), (0, 4), (3, 0), (3, 99), (1, 5), (2, 2), (3, 1)]
 G_HEADS = {
-    1: [(1, 6)],
-    2: [(2, 3)],
-    3: [(3, 1)],
+    1: [(2, 5)],
+    3: [(2, 3)],
     4: [],
-    5: [(3, 2), (0, 8), (1, 7)],
-    7: [(2, 4)],
+    6: [(1, 7)],
+    7: [(3, 3), (2, 4)],
     8: [],
-    9: [(2, 6), (3, 5), (0, 9), (3, 3)],
-    10: [(1, 8)],
+    10: [(2, 6)],
+    11: [(1, 8)],
 }
 G_READY = {
-    0: [(0, 7)],
-    4: [(2, 5)],
+    0: [(0, 6), (1, 3), (0, 7), (1, 4)],
+    4: [(1, 6), (0, 8), (0, 9), (3, 2)],
 }
-G_MERGE = [(3, 4), (2, 7)]
+G_MERGE = [(3, 5), (3, 4), (1, 9)]
 G_FFN = {
-    1: [(3, 6), (2, 8)],
-    4: [(3, 9)],
+    2: [(2, 9)],
 }
 G_FFN_MIDDLE = {
-    0: [(1, 9)],
-    2: [(2, 9), (3, 7), (3, 8)],
+    0: [(2, 7)],
+    1: [(3, 6), (2, 8)],
+    2: [(3, 7)],
+    3: [(3, 8)],
+    4: [(3, 9)],
 }
 R_FFN = {
 }
@@ -420,28 +414,28 @@
     2: [(1, 1)],
     3: [(1, 2)],
     4: [(2, 0), (2, 1), (1, 3)],
-    5: [(1, 4)],
+    5: [(2, 2), (1, 4)],
 }
 R_NORM = {
-    0: [(2, 2)],
+    1: [(3, 0)],
 }
 R_MERGE = []
 R_HEADS = {
-    2: [(2, 4), (1, 5)],
-    4: [(2, 3)],
-    5: [(3, 2)],
-    6: [(2, 5)],
-    7: [(3, 1), (2, 6), (3, 0), (1, 7)],
-    8: [(3, 4)],
-    9: [(1, 8)],
-    11: [(3, 6), (4, 0)],
+    0: [(3, 1), (1, 5)],
+    2: [(3, 2)],
+    3: [(2, 3)],
+    5: [(2, 5)],
+    6: [(3, 3), (1, 7)],
+    8: [(2, 6)],
+    9: [(1, 8), (3, 5)],
+    11: [(2, 7), (3, 6)],
 }
 R_HEADS_END = {
-    3: [(1, 6)],
-    7: [(3, 3)],
+    3: [(2, 4), (1, 6)],
+    7: [(3, 4)],
     11: [(2, 8)],
 }
-R_TAIL = [[(3, 5), (2, 7), (1, 9), (4, 2), (3, 8), (4, 6)], [(4, 5)], [(3, 7), (4, 1), (4, 3), (2, 9), (3, 9), (4, 4), (4, 7), (4, 8)], [(4, 9)]]
+R_TAIL = [[(4, 3), (4, 2), (3, 7), (1, 99), (4, 5), (1, 9), (4, 6), (2, 99), (3, 8), (4, 0), (3, 99), (4, 7), (2, 9), (4, 1), (4, 4)], [], [(3, 9), (4, 8)], [(4, 9)]]
 
 def chosen(width, offset, start=0):
     source = lax.broadcasted_iota(jnp.int32, (LANES, D), 0)
@@ -534,36 +528,47 @@
 
 
 def layer_kernel(
-    bucket, lengths, keeps, x_any, g_any, attend_ref, merge_ref, expand_ref, shrink_ref, pieces_ref,
-    out_any, ig_any, ga_out, gm_out, ge_out, gs_out, vec_out, active_any, slope_any,
-    wa, wm, we, ws, ga, pack, pack_twin, vec_parts, vec_land, vec,
+    bucket, lengths, keeps, x_any, g_any, attend_any, merge_any, expand_any, shrink_any, pieces_any,
+    out_any, ig_any, ga_any, gm_any, ge_any, gs_any, vec_out, active_any, slope_any,
+    attend_ref, merge_ref, expand_ref, shrink_ref, pieces_ref, ge_own, wa, wm, we, ws, ga, pack, pack_twin, vec_parts, vec_land, vec,
     x, g, q, k, v, query_const, key_const, mixed, logsum, xhat, low, xt, lowt, active, slope, first,
-    a0, a1, a3, a4, m0, m1, m3, m4, e0, e1, e2, e3, s0, s1, s3, s4, fa, fm, fe, fs, gain, gain_land,
+    a0, a1, a2, a3, m0, m1, m2, m3, e0, e1, e2, e3, f1, f2, f3, s0, s1, s2, s3, fa, fm, fe, fs, gain, gain_land,
     g_send, g_recv, gt_send, gt_recv, r_send, r_recv, rt_send, rt_recv, own_send, own_recv, vec_send, vec_recv,
     sum_send, sum_recv, last_send, last_recv, local, flow,
 ):
     place = Place()
     c = place.c
     place.greet()
+    shards = [
+        pltpu.make_async_copy(source, target, local.at[4 + n])
+        for n, (source, target) in enumerate(
+            (
+                (expand_any, expand_ref), (pieces_any, pieces_ref), (attend_any, attend_ref), (merge_any, merge_ref),
+                (shrink_any, shrink_ref),
+            )
+        )
+    ]
     x_copy = pltpu.make_async_copy(x_any, x, local.at[0])
     g_copy = pltpu.make_async_copy(g_any, g, local.at[1])
-    x_copy.start()
-    g_copy.start()
-
-    pack[0:HALF, 0 : 3 * D] = attend_ref[...]
-    pack[0:HALF, 3 * D : 4 * D] = merge_ref[...]
-
-    def put_expand(tile, value):
-        pack[0:HALF, 4 * D + LANES * tile : 4 * D + LANES * (tile + 1)] = value.astype(bf16)
-
-    lane_groups(
-        lambda tile: expand_ref[:, LANES * tile : LANES * (tile + 1)].astype(f32), put_expand, ff_moves(False)
-    )
-    place_vectors(place, pieces_ref, vec_parts.at[0])
+    for copy in shards + [x_copy, g_copy]:
+        copy.start()
     token_tables(
         bucket[0], [lengths[0, b] for b in range(SLOTS)], [keeps[0, b] for b in range(SLOTS)],
         query_const, key_const, logsum,
     )
+    for copy in shards:
+        copy.wait()
+
+    pack[0:HALF, 0 : 3 * D] = attend_ref[...]
+    pack[0:HALF, 3 * D : 4 * D] = merge_ref[...]
+
+    def put_expand(tile, value):
+        pack[0:HALF, 4 * D + LANES * tile : 4 * D + LANES * (tile + 1)] = value.astype(bf16)
+
+    lane_groups(
+        lambda tile: expand_ref[:, LANES * tile : LANES * (tile + 1)].astype(f32), put_expand, ff_moves(False)
+    )
+    place_vectors(place, pieces_ref, vec_parts.at[0])
     x_copy.wait()
     xt[...] = x[...].T
     place.met()
@@ -578,30 +583,38 @@
         own_send.at[1], own_recv.at[1], place.twin,
     )
 
-    def vec_copy(source, land, sends, recvs, step, m, peer):
-        return remote(source.at[step], land.at[step + m], sends.at[step + m], recvs.at[step + m], peer)
-
-    def vec_chain(source, land, sends, recvs):
-        steps = [(place.twin,)] + [tuple(peer for _, peer in place.over[a]) for a in "xyz"]
-        return [[vec_copy(source, land, sends, recvs, s, m, p) for m, p in enumerate(peers)] for s, peers in enumerate(steps)]
-
-    vec_steps = vec_chain(vec_parts, vec_land, vec_send, vec_recv)
-    sum_steps = vec_chain(gain, gain_land, sum_send, sum_recv)
-
-    def add_next(steps, source, land, step):
-        steps[step][0].wait_recv()
-        source[step + 1] = (source[step].astype(f32) + land[step].astype(f32)).astype(source.dtype)
-        for copy in steps[step + 1]:
-            copy.start()
-
-    def add_last(steps, source, land):
-        total = source[3].astype(f32)
-        for m, copy in enumerate(steps[3]):
-            copy.wait_recv()
-            total += land[3 + m].astype(f32)
-        return total
-
-    vec_steps[0][0].start()
+    class Sums:
+        def __init__(self, source, land, sends, recvs, order):
+            self.source, self.land, self.steps = source, land, []
+            at = 0
+            for step, peers in enumerate([(place.twin,)] + [tuple(p for _, p in place.over[a]) for a in order]):
+                self.steps.append([])
+                for peer in peers:
+                    copy = remote(source.at[step], land.at[at], sends.at[at], recvs.at[at], peer)
+                    self.steps[-1].append((copy, at))
+                    at += 1
+
+        def run(self, step):
+            if step > 0:
+                total = self.source[step - 1].astype(f32)
+                for copy, at in self.steps[step - 1]:
+                    copy.wait_recv()
+                    total += self.land[at].astype(f32)
+                if step == 4:
+                    return total
+                self.source[step] = total.astype(self.source.dtype)
+            for copy, _ in self.steps[step]:
+                copy.start()
+
+        def finish(self):
+            for copies in self.steps:
+                for copy, _ in copies:
+                    copy.wait_send()
+
+    vec_sums = Sums(vec_parts, vec_land, vec_send, vec_recv, "zxy")
+    grad_sums = Sums(gain, gain_land, sum_send, sum_recv, "xyz")
+
+    vec_sums.run(0)
     own_shrink.start()
 
     def gathers(t):
@@ -617,6 +630,9 @@
 
     def gather_events(names):
         for step, t in names:
+            if t == VECTORS:
+                vec_sums.run(step)
+                continue
             for one in gathers(t):
                 one.run(step)
 
@@ -644,14 +660,8 @@
         )
     ws[place.z, place.y, place.x, my_rows, my_cols] = shrink_ref[:, my_cols]
     own_shrink.wait_recv()
-    gather_events(G_START[:2])
-    add_next(vec_steps, vec_parts, vec_land, 0)
-    gather_events(G_START[2:4])
-    add_next(vec_steps, vec_parts, vec_land, 1)
-    gather_events(G_START[4:8])
-    add_next(vec_steps, vec_parts, vec_land, 2)
-    gather_events(G_START[8:])
-    vec[...] = add_last(vec_steps, vec_parts, vec_land)
+    gather_events(G_START)
+    vec[...] = vec_sums.run(4)
 
     def heads(i, carry):
         when(i, G_HEADS, gather_events)
@@ -769,23 +779,26 @@
     out_copy.start()
 
     def reductions(t):
-        def one(ref, lands, final, cuts, at, *args):
+        def one(ref, land0, lands, final, cuts, at, *args):
             sems = (r_send.at[at], r_recv.at[at], rt_send.at[at], rt_recv.at[at])
-            return Reduce(place, ref, lands, final, cuts(c, *args), cuts(1 - c, *args), sems)
+            return Reduce(place, ref, land0, lands, final, cuts(c, *args), cuts(1 - c, *args), sems)
 
         if t < JOBS:
             j = JOBS - 1 - t
             return [
-                one(we, [e0.at[t % 2], e1.at[t], e2.at[t], e3.at[t], None], fe, expand_cuts, 2 * t, j),
-                one(ws, [s0.at[t % 2], s1.at[t], None, s3.at[t], s4.at[t]], fs, shrink_cuts, 2 * t + 1, j),
+                one(we, e0.at[t % 2], [[ref.at[t] for ref in (e1, e2, e3)], [ref.at[t] for ref in (f1, f2, f3)]], fe, expand_cuts, 2 * t, j),
+                one(ws, s0.at[t % 2], [[ref.at[t] for ref in (s1, s2, s3)]], fs, shrink_cuts, 2 * t + 1, j),
             ]
         if t == JOBS:
-            return [one(wm, [m0, m1, None, m3, m4], fm, merge_cuts, 2 * JOBS)]
+            return [one(wm, m0, [[m1, m2, m3]], fm, merge_cuts, 2 * JOBS)]
         n = t - JOBS - 1
-        return [one(ga, [a0.at[n % 2], a1.at[n], None, a3.at[n], a4.at[n]], fa, attend_cuts, 2 * JOBS + 1 + n, n)]
+        return [one(ga, a0.at[n % 2], [[ref.at[n] for ref in (a1, a2, a3)]], fa, attend_cuts, 2 * JOBS + 1 + n, n)]
 
     def reduce_events(names):
         for step, t in names:
+            if t == VECTORS:
+                grad_sums.run(step)
+                continue
             for one in reductions(t):
                 one.run(step)
 
@@ -873,7 +886,7 @@
         return carry
 
     lax.fori_loop(0, 12, heads_back, 0)
-    sum_steps[0][0].start()
+    grad_sums.run(0)
 
     def last_copy(ref, n, cols, height):
         rows = pl.ds(aligned(height * (1 - c), 8), height)
@@ -891,7 +904,6 @@
         @pl.when(i == 1)
         def _():
             reduce_events(R_TAIL[1])
-            add_next(sum_steps, gain, gain_land, 0)
 
         rows = pl.ds(aligned(i * tile, tile), tile)
         keep = column_of(logsum[rows, :], KEEP_LANE) > 0.0
@@ -904,41 +916,51 @@
     lax.fori_loop(0, T // tile, inputs_part, 0)
     out_ig = pltpu.make_async_copy(first, ig_any, local.at[3])
     out_ig.start()
-    add_next(sum_steps, gain, gain_land, 1)
     reduce_events(R_TAIL[2])
     for copy in early_last + attend_last[:2]:
         copy.start()
-    add_next(sum_steps, gain, gain_land, 2)
     mine, ff_mine = pl.ds(aligned(HALF * c, 8), HALF), pl.ds(aligned(FF_HALF * c, 8), FF_HALF)
     for copy in early_last:
         copy.wait_recv()
-    gm_out[...] = fm[mine, :]
-    gs_out[...] = fs[ff_mine, :]
+    done = [
+        pltpu.make_async_copy(fm.at[mine], gm_any, local.at[4]),
+        pltpu.make_async_copy(fs.at[ff_mine], gs_any, local.at[5]),
+        pltpu.make_async_copy(ge_own, ge_any, local.at[6]),
+    ]
+    done[0].start()
+    done[1].start()
 
     def put_grad(tile, value):
-        ge_out[:, LANES * tile : LANES * (tile + 1)] = value
+        ge_own[:, LANES * tile : LANES * (tile + 1)] = value
 
     lane_groups(lambda tile: fe[mine, LANES * tile : LANES * (tile + 1)], put_grad, ff_moves(True))
+    done[2].start()
     own_pack.wait_send()
     own_shrink.wait_send()
-    for copy in early_last + sum(vec_steps + sum_steps[:3], []):
+    for copy in early_last:
         copy.wait_send()
+    vec_sums.finish()
     for t in range(JOBS + 3):
         for one in reductions(t):
             one.finish()
+    for copy in attend_last[:2]:
+        copy.wait_recv()
+        copy.wait_send()
+    vec_out[...] = own_vectors(place, grad_sums.run(4))
+    grad_sums.finish()
     reduce_events(R_TAIL[3])
     attend_last[2].start()
-    vec_out[...] = own_vectors(place, add_last(sum_steps, gain, gain_land))
-    for copy in sum_steps[3]:
-        copy.wait_send()
     for one in reductions(JOBS + 3):
         one.finish()
-    for copy in attend_last:
-        copy.wait_recv()
-        copy.wait_send()
-    for n in range(3):
-        ga_out[:, D * n : D * n + D] = fa[n, mine, :]
-    out_ig.wait()
+    attend_last[2].wait_recv()
+    done += [
+        pltpu.make_async_copy(fa.at[n, mine], ga_any.at[:, pl.ds(D * n, D)], local.at[7 + n]) for n in range(3)
+    ]
+    for copy in done[3:]:
+        copy.start()
+    attend_last[2].wait_send()
+    for copy in done + [out_ig]:
+        copy.wait()
 
 
 ANY = pl.BlockSpec(memory_space=pl.ANY)
@@ -949,15 +971,18 @@
 def layer_call(buckets, lengths, keeps, inputs, upstream, attend, merge, expand, shrink, pieces):
     dma = pltpu.SemaphoreType.DMA
 
-    def landing(rows, cols, jobs=None, deep=(), slots=None, middle=False):
+    def landing(rows, cols, jobs=None, deep=(), slots=None, parts=1):
         lead = (jobs,) if jobs else ()
-        dims = [((slots,) if slots else lead) + (Z, Y, X), lead + (Z, 2)]
-        dims += [lead + (3, 2), lead + (1,)] if middle else [lead + (3,), lead + (Z,)]
-        return [pltpu.VMEM(d + deep + (rows, cols), bf16) for d in dims]
+        stages = [(Z, 2), (Z,), (3,), (Z, 2), (3, 2), (1,)][: 3 * parts]
+        return [pltpu.VMEM(((slots,) if slots else lead) + (Z, Y, X) + deep + (rows, cols), bf16)] + [
+            pltpu.VMEM(lead + d + deep + (rows, cols // parts), bf16) for d in stages
+        ]
 
     tokens = [pltpu.VMEM((T, D), bf16) for _ in range(5)]
     scratch = (
-        [pltpu.VMEM(*s) for s in WEIGHTS]
+        [pltpu.VMEM(a.shape, a.dtype) for a in (attend, merge, expand, shrink, pieces)]
+        + [pltpu.VMEM((HALF, FF), f32)]
+        + [pltpu.VMEM(*s) for s in WEIGHTS]
         + [
             pltpu.VMEM(*WEIGHTS[0]),
             pltpu.VMEM((32, PACK), bf16),
@@ -982,7 +1007,7 @@
         ]
         + landing(BLOCK, 128, 3, (3,), slots=2)
         + landing(BLOCK, 384)
-        + landing(BLOCK, 256, JOBS, slots=2, middle=True)
+        + landing(BLOCK, 256, JOBS, slots=2, parts=2)
         + landing(SLICE, 384, JOBS, slots=2)
         + [
             pltpu.VMEM((3, BLOCK, D), f32),
@@ -996,7 +1021,7 @@
         + 2 * [dma((2,))]
         + 4 * [dma((6,))]
         + 2 * [dma((5 + JOBS,))]
-        + [dma((4,)), dma((2, 2))]
+        + [dma((10,)), dma((2, 2))]
     )
     return pl.pallas_call(
         layer_kernel,
@@ -1007,8 +1032,8 @@
                 ((FF_HALF, D), f32), ((PIECES, LANES), f32), ((JOBS, T, PART), bf16), ((JOBS, T, PART), bf16),
             )
         ),
-        in_specs=[SM, SM, SM, ANY, ANY, VM, VM, VM, VM, VM],
-        out_specs=[ANY, ANY] + [VM] * 5 + [ANY, ANY],
+        in_specs=[SM] * 3 + [ANY] * 7,
+        out_specs=[ANY] * 6 + [VM] + [ANY] * 2,
         scratch_shapes=scratch,
         compiler_params=pltpu.CompilerParams(collective_id=0, has_side_effects=True, vmem_limit_bytes=VMEM_LIMIT),
         cost_estimate=pl.CostEstimate(flops=60_000_000_000, bytes_accessed=60_000_000, transcendentals=20_000_000),

time: 196 us -> 191 us (0.974)
  Pallas kernels: 192 us -> 187 us
    pallas_call x1, Pallas kernels: 187 us -> 181 us  [layer_call(): pl.pallas_call(layer_kernel, out_shape=tuple((jax.ShapeDtypeStruct(*s) fo...]
where the time goes in v3:
time: 191 us; the launch traced here: 190 us
  Pallas kernels  187 us (98%)
    pallas_call x1, Pallas kernels, layer_call(): pl.pallas_call(layer_kernel, out_shape=tuple((jax.ShapeDtypeStruct(*s) fo...  181 us
    pallas_call x1, Pallas kernels, finish_call(): pl.pallas_call(finish_kernel, out_shape=tuple((jax.ShapeDtypeStruct(*s) f...  5.7 us

profile of v3, /device:TPU:0, one launch (start us, length us, event | category | flops | bytes accessed | tf_op | source)
XLA Modules:
  0.0 189.9 jit_solution(16763046100974772726)
XLA Ops:
  1.3 1.3 convert_add_fusion.pieces_any
  2.6 181.4 %shard_map.238 = (bf16[1024,768]{1,0:T(8,128)(2,1)}, f32[1024,768]{1,0:T(8,128)}, f32[24,2304]{1,0:T(8,128)}, f32[24,768]{1,0:T(8,128)}, f32[24,3072]{1,0:T(8,12...) custom-call(s32[1]{0:T(128)S(6)} %copy.27.bucket, ...), custom_call_target="tpu_custom_call" | custom-call | flops 60000002048 | bytes 60000000 | tf_op jit(solution)/shard_map/pallas_call | solution.py:1026
  184.1 5.7 %shard_map.239 = (f32[1024,768]{1,0:T(8,128)}, bf16[1024,768]{1,0:T(8,128)(2,1)}, f32[24,2304]{1,0:T(8,128)}, f32[24,768]{1,0:T(8,128)}, f32[24,3072]{1,0:T(8,12...) custom-call(f32[1024,768]{1,0:T(8,128)} %get-tuple-element.31.refs_0, ...), custom_call_target="tpu_custom_call" | custom-call | tf_op jit(solution)/shard_map/pallas_call | solution.py:1086

commit v4 on v3

--- a/solution.py
+++ b/solution.py
@@ -381,29 +381,30 @@
 )
 VMEM_LIMIT = 255 * 2**18
 
-G_START = [(0, 0), (0, 1), (0, 2), (1, 99), (1, 0), (1, 1), (2, 0), (0, 5), (0, 3), (1, 2), (2, 99), (2, 1), (0, 4), (3, 0), (3, 99), (1, 5), (2, 2), (3, 1)]
+G_START = [(0, 0), (0, 3), (1, 99), (1, 0), (0, 1), (1, 3), (0, 2), (2, 0), (2, 99), (2, 3), (0, 5), (1, 1), (0, 4), (0, 6), (3, 0), (3, 99), (1, 2)]
 G_HEADS = {
-    1: [(2, 5)],
-    3: [(2, 3)],
-    4: [],
-    6: [(1, 7)],
-    7: [(3, 3), (2, 4)],
+    1: [(1, 4)],
+    2: [(0, 7), (3, 1)],
+    3: [(1, 6)],
+    4: [(0, 8), (2, 5)],
+    5: [(3, 2)],
+    6: [(2, 4)],
     8: [],
-    10: [(2, 6)],
-    11: [(1, 8)],
+    10: [(0, 9), (2, 6)],
+    11: [(3, 5)],
 }
 G_READY = {
-    0: [(0, 6), (1, 3), (0, 7), (1, 4)],
-    4: [(1, 6), (0, 8), (0, 9), (3, 2)],
+    0: [(2, 1), (1, 5), (2, 2), (3, 3)],
+    8: [(1, 7)],
 }
-G_MERGE = [(3, 5), (3, 4), (1, 9)]
+G_MERGE = [(3, 4), (1, 8)]
 G_FFN = {
-    2: [(2, 9)],
+    2: [(2, 8)],
 }
 G_FFN_MIDDLE = {
     0: [(2, 7)],
-    1: [(3, 6), (2, 8)],
-    2: [(3, 7)],
+    1: [(3, 6), (1, 9)],
+    2: [(3, 7), (2, 9)],
     3: [(3, 8)],
     4: [(3, 9)],
 }
@@ -414,28 +415,27 @@
     2: [(1, 1)],
     3: [(1, 2)],
     4: [(2, 0), (2, 1), (1, 3)],
-    5: [(2, 2), (1, 4)],
+    5: [(1, 4)],
 }
 R_NORM = {
-    1: [(3, 0)],
+    1: [(3, 0), (2, 2), (1, 5)],
 }
 R_MERGE = []
 R_HEADS = {
-    0: [(3, 1), (1, 5)],
-    2: [(3, 2)],
-    3: [(2, 3)],
-    5: [(2, 5)],
-    6: [(3, 3), (1, 7)],
+    1: [(2, 3)],
+    2: [(3, 1)],
+    3: [(2, 4)],
+    5: [(1, 6)],
+    6: [(2, 5), (3, 3)],
+    7: [(3, 4), (1, 7)],
     8: [(2, 6)],
     9: [(1, 8), (3, 5)],
     11: [(2, 7), (3, 6)],
 }
 R_HEADS_END = {
-    3: [(2, 4), (1, 6)],
-    7: [(3, 4)],
-    11: [(2, 8)],
+    3: [(3, 2)],
 }
-R_TAIL = [[(4, 3), (4, 2), (3, 7), (1, 99), (4, 5), (1, 9), (4, 6), (2, 99), (3, 8), (4, 0), (3, 99), (4, 7), (2, 9), (4, 1), (4, 4)], [], [(3, 9), (4, 8)], [(4, 9)]]
+R_TAIL = [[(2, 8), (4, 1), (3, 7), (1, 99), (1, 9), (4, 3)], [(3, 8), (2, 99)], [(3, 99), (2, 9), (4, 0), (4, 4), (4, 7), (3, 9), (4, 6), (4, 5), (4, 2), (4, 8)], [(4, 9)]]
 
 def chosen(width, offset, start=0):
     source = lax.broadcasted_iota(jnp.int32, (LANES, D), 0)

time: 191 us -> 187 us (0.979)
  Pallas kernels: 187 us -> 183 us
    pallas_call x1, Pallas kernels: 181 us -> 177 us  [layer_call(): pl.pallas_call(layer_kernel, out_shape=tuple((jax.ShapeDtypeStruct(*s) fo...]
where the time goes in v4:
time: 187 us; the launch traced here: 186 us
  Pallas kernels  183 us (98%)
    pallas_call x1, Pallas kernels, layer_call(): pl.pallas_call(layer_kernel, out_shape=tuple((jax.ShapeDtypeStruct(*s) fo...  177 us
    pallas_call x1, Pallas kernels, finish_call(): pl.pallas_call(finish_kernel, out_shape=tuple((jax.ShapeDtypeStruct(*s) f...  5.7 us

profile of v4, /device:TPU:0, one launch (start us, length us, event | category | flops | bytes accessed | tf_op | source)
XLA Modules:
  0.0 185.8 jit_solution(11642552595505764363)
XLA Ops:
  1.3 1.3 convert_add_fusion.pieces_any
  2.6 177.2 %shard_map.238 = (bf16[1024,768]{1,0:T(8,128)(2,1)}, f32[1024,768]{1,0:T(8,128)}, f32[24,2304]{1,0:T(8,128)}, f32[24,768]{1,0:T(8,128)}, f32[24,3072]{1,0:T(8,12...) custom-call(s32[1]{0:T(128)S(6)} %copy.27.bucket, ...), custom_call_target="tpu_custom_call" | custom-call | flops 60000002048 | bytes 60000000 | tf_op jit(solution)/shard_map/pallas_call | solution.py:1026
  179.9 5.7 %shard_map.239 = (f32[1024,768]{1,0:T(8,128)}, bf16[1024,768]{1,0:T(8,128)(2,1)}, f32[24,2304]{1,0:T(8,128)}, f32[24,768]{1,0:T(8,128)}, f32[24,3072]{1,0:T(8,12...) custom-call(f32[1024,768]{1,0:T(8,128)} %get-tuple-element.31.refs_0, ...), custom_call_target="tpu_custom_call" | custom-call | tf_op jit(solution)/shard_map/pallas_call | solution.py:1086

commit v5 on v4

--- a/solution.py
+++ b/solution.py
@@ -552,10 +552,6 @@
     g_copy = pltpu.make_async_copy(g_any, g, local.at[1])
     for copy in shards + [x_copy, g_copy]:
         copy.start()
-    token_tables(
-        bucket[0], [lengths[0, b] for b in range(SLOTS)], [keeps[0, b] for b in range(SLOTS)],
-        query_const, key_const, logsum,
-    )
     for copy in shards:
         copy.wait()
 
@@ -569,8 +565,6 @@
         lambda tile: expand_ref[:, LANES * tile : LANES * (tile + 1)].astype(f32), put_expand, ff_moves(False)
     )
     place_vectors(place, pieces_ref, vec_parts.at[0])
-    x_copy.wait()
-    xt[...] = x[...].T
     place.met()
 
     own_pack = remote(pack, pack_twin, own_send.at[0], own_recv.at[0], place.twin)
@@ -660,7 +654,14 @@
         )
     ws[place.z, place.y, place.x, my_rows, my_cols] = shrink_ref[:, my_cols]
     own_shrink.wait_recv()
-    gather_events(G_START)
+    gather_events(G_START[:3])
+    token_tables(
+        bucket[0], [lengths[0, b] for b in range(SLOTS)], [keeps[0, b] for b in range(SLOTS)],
+        query_const, key_const, logsum,
+    )
+    x_copy.wait()
+    xt[...] = x[...].T
+    gather_events(G_START[3:])
     vec[...] = vec_sums.run(4)
 
     def heads(i, carry):

time: 187 us -> 187 us (level)
  no operation moved by 1% of the time
where the time goes in v5:
time: 187 us
  Pallas kernels  184 us (98%)
    pallas_call x1, Pallas kernels, layer_call(): pl.pallas_call(layer_kernel, out_shape=tuple((jax.ShapeDtypeStruct(*s) fo...  178 us
    pallas_call x1, Pallas kernels, finish_call(): pl.pallas_call(finish_kernel, out_shape=tuple((jax.ShapeDtypeStruct(*s) f...  5.7 us

profile of v5, /device:TPU:0, one launch (start us, length us, event | category | flops | bytes accessed | tf_op | source)
XLA Modules:
  0.0 186.6 jit_solution(4373957492608005946)
XLA Ops:
  1.3 1.3 convert_add_fusion.pieces_any
  2.6 178.0 %shard_map.238 = (bf16[1024,768]{1,0:T(8,128)(2,1)}, f32[1024,768]{1,0:T(8,128)}, f32[24,2304]{1,0:T(8,128)}, f32[24,768]{1,0:T(8,128)}, f32[24,3072]{1,0:T(8,12...) custom-call(s32[1]{0:T(128)S(6)} %copy.27.bucket, ...), custom_call_target="tpu_custom_call" | custom-call | flops 60000002048 | bytes 60000000 | tf_op jit(solution)/shard_map/pallas_call | solution.py:1027
  180.7 5.7 %shard_map.239 = (f32[1024,768]{1,0:T(8,128)}, bf16[1024,768]{1,0:T(8,128)(2,1)}, f32[24,2304]{1,0:T(8,128)}, f32[24,768]{1,0:T(8,128)}, f32[24,3072]{1,0:T(8,12...) custom-call(f32[1024,768]{1,0:T(8,128)} %get-tuple-element.31.refs_0, ...), custom_call_target="tpu_custom_call" | custom-call | tf_op jit(solution)/shard_map/pallas_call | solution.py:1087
